TPU v7x, 32 devices: a whole 2x2x4 slice. The times are simulated.
32 devices in a mesh: dp: 8 (over y, x, core), mp: 4 (over z).
Axes of the slice: x: 2, y: 2, z: 4, core: 2. Of those that a mesh axis runs over, the one named last changes fastest.
Arguments:
- tokens: bfloat16 [32768, 512], P(('dp', 'mp')), may hold values from -6 to 6
- cotangent: bfloat16 [32768, 512], P(('dp', 'mp')), may hold values from -13.5 to 13.5
- master: float32 [4, 64, 128, 128], P('mp', 'dp'), may hold values from -0.2165625 to 0.2165625
- moment_one: float32 [4, 64, 128, 128], P('mp', 'dp'), may hold values from -615.46574 to 615.46574
- moment_two: float32 [4, 64, 128, 128], P('mp', 'dp'), may hold values from 838.8608 to 94699.52
- basis_left: float32 [4, 64, 128, 128], P('mp', 'dp'), may hold values from -1 to 1, as said below
- basis_right: float32 [4, 64, 128, 128], P('mp', 'dp'), may hold values from -1 to 1, as said below
- owner: int32 [64], replicated, may hold values from 0 to 7, as said below
- gains: float32 [2, 512], replicated, may hold values from 0.5 to 1.5
- gain_moment_one: float32 [2, 512], replicated, may hold values from -470.65027 to 470.65027
- gain_moment_two: float32 [2, 512], replicated, may hold values from 13844.48 to 55377.92
Outputs:
- block_out: bfloat16 [32768, 512], P(('dp', 'mp'))
- input_grad: float32 [32768, 512], P(('dp', 'mp'))
- moment_one_new: float32 [4, 64, 128, 128], P('mp', 'dp')
- moment_two_new: float32 [4, 64, 128, 128], P('mp', 'dp')
- master_new: float32 [4, 64, 128, 128], P('mp', 'dp')
- master_low: bfloat16 [4, 64, 128, 128], P('mp', 'dp')
- gain_moment_one_new: float32 [2, 512], replicated
- gain_moment_two_new: float32 [2, 512], replicated
- gains_new: float32 [2, 512], replicated
- forget_mean: float32 [], replicated
Inputs may be any that keep to these rules, and one draw needn't show every extreme that they name: `owner`: every index of dp appears exactly 64 * 4 / 32 times. `basis_left`: every [128, 128] block is an orthogonal matrix. `basis_right`: every [128, 128] block is an orthogonal matrix.
All inputs are finite; a program needn't handle non-finite values.
Results may differ from a plain program's by a relative error of at most 0.0079.
Values may be sent and summed in bfloat16 or wider, within the bound.
A program may use at most 192 MiB of HBM per device.

v0:
```python
import functools

import jax
import jax.numpy as jnp
from jax import lax
from jax.experimental import pallas as pl
from jax.experimental.pallas import tpu as pltpu
from jax.sharding import PartitionSpec as P

D = 512
H = 1024
FF = 2048
BLK = 128
STEP = 10
L = 1024

norm_eps = 1e-05
beta_one = 0.5
beta_two = 0.5
adam_eps = 1e-08
learn_rate = 0.02
gain_rate = 0.1
weight_decay = 0.1
highest = lax.Precision.HIGHEST

f32 = jnp.float32
bf16 = jnp.bfloat16
SUB = 8
J = L // SUB
R = 128


def dot(a, b, trans_b=False):
    dims = (((1,), (1,)), ((), ())) if trans_b else (((1,), (0,)), ((), ()))
    return lax.dot_general(a, b, dims, preferred_element_type=f32)


def recip(v):
    return pltpu.reciprocal(v, approx=True)


def sigmoid(v):
    return recip(1.0 + jnp.exp(-v))


def shift_down(v):
    rolled = pltpu.roll(v, 1, 0)
    row = lax.broadcasted_iota(jnp.int32, v.shape, 0)
    return jnp.where(row == 0, 0.0, rolled)


def shift_up(v):
    rolled = pltpu.roll(v, SUB - 1, 0)
    row = lax.broadcasted_iota(jnp.int32, v.shape, 0)
    return jnp.where(row == SUB - 1, 0.0, rolled)


def gelu_terms(x):
    a = jnp.abs(x)
    t = recip(1.0 + a * (0.3275911 * 0.7071067811865476))
    poly = t * (
        0.5 * 0.254829592
        + t
        * (
            0.5 * -0.284496736
            + t * (0.5 * 1.421413741 + t * (0.5 * -1.453152027 + t * (0.5 * 1.061405429)))
        )
    )
    e = jnp.exp(x * x * -0.5)
    tail = poly * e
    cdf = jnp.where(x < 0.0, tail, 1.0 - tail)
    return cdf, x * e * 0.3989422804014327


MESH = pl.DeviceIdType.MESH


class Copy:
    def __init__(self, net, make):
        self.net, self.make = net, make

    def start(self):
        self.net.open.append(self)
        self.make().start()
        return self

    def wait_recv(self):
        self.make().wait_recv()

    def wait_send(self):
        self.make().wait_send()


class Exchange:
    def __init__(self, send, recv):
        self.send, self.recv, self.known, self.used, self.open = send, recv, {}, 0, []

    def copy(self, parts, key=None):
        if key in self.known:
            return self.known[key]
        k = self.used
        self.used += 1

        def make():
            src, dst, device = parts()
            return pltpu.make_async_remote_copy(
                src_ref=src,
                dst_ref=dst,
                send_sem=self.send.at[k],
                recv_sem=self.recv.at[k],
                device_id=device,
                device_id_type=MESH,
            )

        copy = Copy(self, make)
        if key is not None:
            self.known[key] = copy
        return copy

    def start(self, parts):
        return self.copy(parts).start()

    def drain(self):
        for copy in self.open:
            copy.wait_send()
        self.open = []


class Gather:
    def __init__(self, net, master, rank, slots, pool, weights, free):
        self.net, self.weights, self.rank, self.free = net, weights, rank, free
        self.held = [slots, *pool]
        d, m = lax.axis_index("dp"), lax.axis_index("mp")
        core, col, row = d % 2, (d // 2) % 2, d // 4
        self.me, self.m, self.side = d, m, core
        self.core = d + 1 - 2 * core
        self.plane = [d + 2 - 4 * col, d + 4 - 8 * row, d + 6 - 4 * col - 8 * row]
        self.order = [m, m + 1 - 2 * (m % 2), m + 2 - 4 * (m // 2), 3 - m]
        self.peers = [(e, m) for e in [self.core] + self.plane] + [(d, k) for k in self.order[1:]]
        barrier = pltpu.get_barrier_semaphore()
        for device in self.peers:
            pl.semaphore_signal(barrier, inc=1, device_id=device, device_id_type=MESH)
        self.n = master.shape[0]
        for s in range(self.n):
            slots[d * self.n + s] = master[s].astype(bf16)
        pl.semaphore_wait(barrier, len(self.peers))

    def rows(self, i, e, first, count):
        return self.held[i].at[pl.ds(e * self.n + first, count)]

    def along(self, i, e):
        return self.net.copy(
            lambda: (self.rows(0, e, 0, self.n), self.rows(i, e, 0, self.n), (self.me, self.order[i])),
            ("along", i, e is self.me),
        )

    def within(self, key, i, e, first, count, to):
        return self.net.copy(
            lambda: (self.rows(i, e, first, count), self.rows(i, e, first, count), (to, self.m)), (key, i)
        )

    def first(self, i):
        (x, y, _), h = self.plane, self.n // 2
        if i == 1:
            jobs = ((0, self.n, x), (0, self.n, y))
        else:
            jobs = ((0, h, x), (h, h, y), (h, h, x), (0, h, y))
        return [self.within(("first", k), i, self.me, *job) for k, job in enumerate(jobs)]

    def last(self, i):
        x, y, z = self.plane
        if i == 1:
            return [self.along(1, z)]
        h = self.n // 2
        return [self.within("over y", i, x, 0, h, y), self.within("over x", i, y, h, h, x)]

    def inside(self, i):
        return [self.within(("inside", k), i, e, 0, self.n, self.core) for k, e in enumerate([self.me] + self.plane)]

    def along_start(self, i):
        self.along(i, self.me).start()

    def across_start(self):
        self.last(1)[0].start()

    def start(self, i):
        if i:
            self.along(i, self.me).wait_recv()
        for copy in self.first(i):
            copy.start()
        self.inside(i)[0].start()

    def forward(self, i):
        if i == 1:
            return
        for came, copy in zip(self.first(i), self.last(i)):
            came.wait_recv()
            copy.start()

    def pair(self, i):
        for came, copy in zip(self.first(i)[-2:], self.inside(i)[1:3]):
            came.wait_recv()
            copy.start()
        for came in self.last(i):
            came.wait_recv()
        self.inside(i)[3].start()

    def ready(self, i):
        for copy in self.inside(i):
            copy.wait_recv()

    def place(self, i):
        wg, wo, wu, wd = self.weights
        row_tiles, gates = D // BLK, wg.shape[2] // BLK
        cols, outs = gates + wu.shape[2] // BLK, wo.shape[1] // BLK
        for b in range(row_tiles * cols + (wo.shape[1] + wd.shape[1]) // BLK * row_tiles):
            if b < row_tiles * cols:
                r, c = b // cols, b % cols
                ref = wg if c < gates else wu
                c -= 0 if c < gates else gates
            else:
                r, c = (b - row_tiles * cols) // row_tiles, (b - row_tiles * cols) % row_tiles
                ref = wo if r < outs else wd
                r -= 0 if r < outs else outs
            block = self.held[i][self.rank[b]]
            ref[self.order[i], r * BLK : (r + 1) * BLK, c * BLK : (c + 1) * BLK] = block

    def done(self):
        for device in self.peers:
            pl.semaphore_signal(self.free, inc=1, device_id=device, device_id_type=MESH)

    def all_done(self):
        pl.semaphore_wait(self.free, len(self.peers))


def stack_places(hm, fm):
    row_tiles, gates, ups, outs = D // BLK, 3 * hm // BLK, fm // BLK, hm // BLK
    cols = gates + ups
    first_down = row_tiles * ups
    first_out = 2 * first_down
    first_gate = first_out + row_tiles * outs
    table = []
    for b in range(row_tiles * (cols + outs + ups)):
        if b < row_tiles * cols:
            r, c = b // cols, b % cols
            table.append(first_gate + r * gates + c if c < gates else r * ups + c - gates)
        else:
            k = b - row_tiles * cols
            table.append(first_out + k if k < row_tiles * outs else first_down + k - row_tiles * outs)
    return ((0, first_out), (first_out, row_tiles * outs), (first_gate, row_tiles * gates)), table


UPDOWN, OUT, GATE = range(3)


class Reduce:
    def __init__(self, net, gather, grads, units, pool):
        self.net, self.g, self.grads, self.units, self.pool = net, gather, grads, units, pool
        self.half = grads.shape[1] // 2
        self.eighth = grads.shape[1] // 8
        self.copies = {}

    def place(self, e):
        return (e % 2) * 4 + e // 2

    def inside(self, unit, i):
        g, (first, count) = self.g, self.units[unit]
        return self.net.copy(
            lambda: (
                self.grads.at[g.order[i], pl.ds(first + (1 - g.side) * (count // 2), count // 2)],
                self.pool[i - 1].at[pl.ds(first // 2, count // 2)],
                (g.core, g.m),
            ),
            ("chip", unit, i),
        )

    def chip(self, unit, i):
        self.inside(unit, i).start()

    def spot(self, unit, i, slot, first, count):
        base, total = self.units[unit]
        return self.pool[i - 1].at[pl.ds(self.half + slot * self.eighth + base // 8 + first, count)]

    def parts(self, unit, i):
        n = self.units[unit][1] // 8
        if i == 1:
            return ((0, n),)
        h = (n + i % 2) // 2 if n % 2 else n // 2
        return (0, h), (h, n - h)

    def share(self, unit, i, e, first, count):
        base, total = self.units[unit]
        return self.grads.at[self.g.order[i], pl.ds(base + self.place(e) * (total // 8) + first, count)]

    def send(self, unit, i, e, part, slot, to):
        if part[1]:
            self.copies[1, unit, i, slot, part] = self.net.start(
                lambda: (self.share(unit, i, e, *part), self.spot(unit, i, slot, *part), (to, self.g.m))
            )

    def take(self, unit, i, slot, part):
        self.copies[1, unit, i, slot, part].wait_recv()
        return self.spot(unit, i, slot, *part)[...].astype(f32)

    def plane(self, unit, i):
        g, (first, count) = self.g, self.units[unit]
        x, y, z = g.plane
        self.inside(unit, i).wait_recv()
        m = g.order[i]
        start, came = first + g.side * (count // 2), self.pool[i - 1]

        @pl.loop(0, count // 2)
        def _(b):
            total = self.grads[m, start + b].astype(f32) + came[first // 2 + b].astype(f32)
            self.grads[m, start + b] = total.astype(bf16)

        if i == 1:
            (whole,) = self.parts(unit, i)
            self.send(unit, i, x, whole, 1, x)
            self.send(unit, i, y, whole, 2, y)
            self.copies[3, unit] = self.net.start(
                lambda: (self.share(unit, i, z, *whole), self.spot(unit, i, 0, *whole), (g.me, g.order[i]))
            )
            return
        one, two = self.parts(unit, i)
        self.send(unit, i, z, one, 0, x)
        self.send(unit, i, z, two, 0, y)
        self.send(unit, i, x, one, 1, x)
        self.send(unit, i, y, two, 2, y)

    def turn(self, unit, i):
        if i == 1:
            return
        x, y, z = self.g.plane
        for part, slot, e in zip(self.parts(unit, i), (2, 1), (y, x)):
            if part[1]:
                ref = self.share(unit, i, e, *part)
                ref[...] = (ref[...].astype(f32) + self.take(unit, i, 0, part)).astype(bf16)
                self.send(unit, i, e, part, slot, e)

    def model(self, unit, i):
        g, (first, count) = self.g, self.units[unit]
        n = count // 8
        for part in self.parts(unit, i):
            if part[1]:
                ref = self.share(unit, i, g.me, *part)
                total = ref[...].astype(f32) + self.take(unit, i, 1, part) + self.take(unit, i, 2, part)
                ref[...] = total.astype(bf16)
        self.copies[2, unit, i] = self.net.start(
            lambda: (self.share(unit, i, g.me, 0, n), self.spot(unit, i, 3, 0, n), (g.me, g.order[i]))
        )

    def own(self, unit):
        g, (first, count) = self.g, self.units[unit]
        n = count // 8
        rows = pl.ds(first + self.place(g.me) * n, n)
        total = self.grads[g.m, rows].astype(f32)
        for i in (1, 2, 3):
            self.copies[2, unit, i].wait_recv()
            total += self.pool[i - 1][pl.ds(self.half + 3 * self.eighth + first // 8, n)].astype(f32)
        self.grads[g.m, rows] = total.astype(bf16)
        self.copies[3, unit].wait_recv()
        rows = pl.ds(first + self.place(g.plane[2]) * n, n)
        total = self.grads[g.m, rows].astype(f32) + self.spot(unit, 1, 0, 0, n)[...].astype(f32)
        self.grads[g.m, rows] = total.astype(bf16)

    def into_slots(self, out, slot_place, e):
        n = self.eighth
        for k in range(n):
            out[self.place(e) * n + k] = self.grads[self.g.m, slot_place[e * n + k]]

    def slots_chip(self, out, slot_place, pair):
        g, n = self.g, self.eighth
        self.last = []
        targets = (g.plane[2], g.plane[0], g.plane[1], g.me)
        for e in targets:
            other = e + 1 - 2 * g.side
            self.into_slots(out, slot_place, other)
            self.last.append(
                self.net.start(
                    lambda e=e, other=other: (
                        out.at[pl.ds(self.place(other) * n, n)],
                        pair.at[pl.ds((e // 2) * n, n)],
                        (g.core, g.m),
                    )
                )
            )
        for e in targets:
            self.into_slots(out, slot_place, e)

    def slots_plane(self, out, pair, far):
        g, n = self.g, out.shape[0] // 8
        h = n // 2
        x, y, z = g.plane
        wait = dict(zip("zxyo", self.last))

        def mine(e, first, count):
            return pl.ds((g.side * 4 + e // 2) * n + first, count)

        def join(e):
            rows = mine(e, 0, n)
            out[rows] = (out[rows].astype(f32) + pair[pl.ds((e // 2) * n, n)].astype(f32)).astype(bf16)

        def send(e, first, slot, to):
            return self.net.start(lambda: (out.at[mine(e, first, h)], far.at[slot], (to, g.m)))

        wait["z"].wait_recv()
        join(z)
        over_x = send(z, 0, 0, x)
        over_y = send(z, h, 1, y)
        wait["x"].wait_recv()
        join(x)
        self.ends = [send(x, 0, 2, x)]
        wait["y"].wait_recv()
        join(y)
        self.ends.append(send(y, h, 3, y))
        over_x.wait_recv()
        rows = mine(y, 0, h)
        out[rows] = (out[rows].astype(f32) + far[0].astype(f32)).astype(bf16)
        self.ends.append(send(y, 0, 4, y))
        over_y.wait_recv()
        rows = mine(x, h, h)
        out[rows] = (out[rows].astype(f32) + far[1].astype(f32)).astype(bf16)
        self.ends.append(send(x, h, 5, x))
        wait["o"].wait_recv()

    def slots_end(self, out, pair, far, owned):
        g, n = self.g, out.shape[0] // 8
        h = n // 2
        for copy in self.ends:
            copy.wait_recv()
        for first, slots in ((0, (2, 4)), (h, (3, 5))):
            total = out[pl.ds((g.side * 4 + g.me // 2) * n + first, h)].astype(f32)
            total += pair[pl.ds((g.me // 2) * n + first, h)].astype(f32)
            for k in slots:
                total += far[k].astype(f32)
            owned[first : first + h] = total


class SmallSum:
    def __init__(self, net, gather, values, along, across, inside):
        self.net, self.g, self.values = net, gather, values
        self.slots = (along, across, inside)
        self.peers = (
            [(gather.me, k) for k in gather.order[1:]],
            [(e, gather.m) for e in gather.plane],
            [(gather.core, gather.m)],
        )
        self.mine = (gather.m, gather.me // 2, gather.side)
        self.open = []

    def send(self, stage):
        slot = self.slots[stage]
        slot[self.mine[stage]] = self.values[...]
        ref = slot.at[self.mine[stage]]
        self.open = [self.net.start(lambda peer=peer: (ref, ref, peer)) for peer in self.peers[stage]]

    def add(self, stage):
        for copy in self.open:
            copy.wait_recv()
        slot = self.slots[stage]
        total = slot[0]
        for k in range(1, slot.shape[0]):
            total += slot[k]
        self.values[...] = total


def compute_kernel(linked, *refs):
    if linked:
        tokens, cotangent, master, rank, slot_place, gains = refs[:6]
        block_out, input_grad, owned, small = refs[6:10]
        wg, wo, wu, wd, grads, slots, *pool, pair, far, sum_a, sum_b, sum_c, send, recv, free = refs[10:27]
        scratch = refs[27:]
    else:
        tokens, cotangent, base, wg, wo, wu, wd, gains = refs[:8]
        block_out, input_grad, grads, small = refs[8:12]
        scratch = refs[12:]
    (n1, n1t, cot, cott, n2, n2t, forget, admit, cand, state, scan, acc_a, acc_b, mixed, mid, kept, fills, tally, local) = scratch
    dml, dmlt = n2, n2t
    parts, _, hm3 = wg.shape
    hm = hm3 // 3
    fm = wu.shape[2]
    units, _ = stack_places(hm, fm)
    act, dup, dpre = mid.at[:, :fm], mid.at[:, fm:], mid.at[:, : 3 * hm]
    gain_one = gains[0:1, :]
    gain_two = gains[1:2, :]

    fetch_cot = pltpu.make_async_copy(cotangent, cot, local.at[0])
    fetch_tok = pltpu.make_async_copy(tokens, n1, local.at[1])
    fetch_tok.start()
    fetch_cot.start()

    column_halves = (slice(0, D // 2), slice(D // 2, D))

    def stack(m, first, wide, left, value):
        for r in range(value.shape[0] // BLK):
            for c in range(value.shape[1] // BLK):
                grads[m, first + r * wide + left + c] = value[r * BLK : (r + 1) * BLK, c * BLK : (c + 1) * BLK].astype(bf16)

    def stack_turned(m, first, value):
        high = value.shape[0] // BLK
        for r in range(high):
            for c in range(value.shape[1] // BLK):
                grads[m, first + c * high + r] = value[r * BLK : (r + 1) * BLK, c * BLK : (c + 1) * BLK].astype(bf16)

    def permute_in(src, dst):
        for k in range(D // BLK):
            scan[k] = src[:, k * BLK : (k + 1) * BLK].astype(f32)

        @pl.loop(0, J // 2, unroll=4)
        def _(j):
            for k in range(D // BLK):
                lo = scan[k, pl.ds(2 * j, SUB, stride=J), :]
                hi = scan[k, pl.ds(2 * j + 1, SUB, stride=J), :]
                dst[pl.ds(pl.multiple_of(16 * j, 16), 16), k * BLK : (k + 1) * BLK] = jnp.concatenate([lo, hi], 0).astype(bf16)

    def permute_out(src, dst):
        @pl.loop(0, J, unroll=4)
        def _(j):
            rows = pl.ds(pl.multiple_of(j * SUB, SUB), SUB)
            for k in range(D // BLK):
                scan[k, pl.ds(j, SUB, stride=J), :] = src[rows, k * BLK : (k + 1) * BLK]

        for k in range(D // BLK):
            dst[:, k * BLK : (k + 1) * BLK] = scan[k].astype(dst.dtype)

    def put(first, rows, value):
        for k in range(hm // BLK):
            scan[first + k, rows, :] = value[:, k * BLK : (k + 1) * BLK]

    def take(first, rows):
        return jnp.concatenate([scan[first + k, rows, :] for k in range(hm // BLK)], 1)

    half = hm // BLK

    def spread(v):
        return jnp.broadcast_to(v[None], (R // SUB, SUB, hm)).reshape(R, hm)


    if linked:
        net = Exchange(send, recv)
        gather = Gather(net, master, rank, slots, pool, (wg, wo, wu, wd), free)
        gather.start(0)
        gather.along_start(1)
        reduce = Reduce(net, gather, grads, units, pool)

    def of_turn(t):
        if not linked:
            return t
        high, low = gather.m // 2, gather.m % 2
        t_high, t_low = t // 2, t % 2
        return 2 * (high + t_high - 2 * high * t_high) + low + t_low - 2 * low * t_low

    fetch_tok.wait()
    permute_in(n1, n1)
    mixed[...] = n1[...].astype(f32)

    @pl.loop(0, L // R)
    def _(i):
        rows = pl.ds(pl.multiple_of(i * R, R), R)
        x = mixed[rows, :]
        r = lax.rsqrt(jnp.mean(x * x, axis=-1, keepdims=True) + norm_eps)
        n1[rows, :] = (x * r * gain_one).astype(bf16)

    n1t[...] = n1[...].T

    if linked:
        gather.forward(0)
        gather.along_start(2)
        gather.along_start(3)
    fetch_cot.wait()
    permute_in(cot, cot)
    if linked:
        gather.start(1)
        gather.pair(0)
        gather.across_start()
    cott[...] = cot[...].T

    fills[0] = jnp.zeros((SUB, hm), f32)
    fills[1] = jnp.ones((SUB, hm), f32)
    tally[0] = fills[0]
    tally[1] = fills[0]

    @pl.loop(0, parts)
    def _(turn):
        m = of_turn(turn)
        if linked:
            for k in range(parts):

                @pl.when(turn == k)
                def _():
                    if k:
                        gather.pair(k)
                    gather.ready(k)
                    gather.place(k)

        forget[m] = dot(n1[...], wg[m, :, :hm])
        admit[m] = dot(n1[...], wg[m, :, hm : 2 * hm])
        cand[m] = dot(n1[...], wg[m, :, 2 * hm :])

        if linked:
            for k in range(parts - 1):

                @pl.when(turn == k)
                def _():
                    if k:
                        gather.forward(k + 1)
                    if k < 2:
                        gather.start(k + 2)

        @pl.loop(0, L // R)
        def _(i):
            rows = pl.ds(pl.multiple_of(i * R, R), R)
            f = sigmoid(forget[m, rows, :])
            a = sigmoid(admit[m, rows, :])
            inv = recip(f + a)
            forget[m, rows, :] = f
            admit[m, rows, :] = a
            kept[rows, :] = f * inv
            put(0, rows, a * inv * cand[m, rows, :])

        def step(j, carry):
            s, p, k_sum, kj_sum = carry
            rows = pl.ds(pl.multiple_of(j * SUB, SUB), SUB)
            keep = kept[rows, :]
            s = keep * s + take(0, rows)
            p = keep * p
            put(0, rows, s)
            put(half, rows, p)
            return s, p, k_sum + keep, kj_sum + keep * j.astype(f32)

        s, p, k_sum, kj_sum = lax.fori_loop(0, J, step, (fills[0], fills[1], fills[0], fills[0]), unroll=16)
        tally[0] += k_sum
        tally[1] += kj_sum
        enter = fills[0]
        for _ in range(SUB - 1):
            enter = shift_down(s + p * enter)

        @pl.loop(0, L // R)
        def _(i):
            rows = pl.ds(pl.multiple_of(i * R, R), R)
            state[m, pl.ds(pl.multiple_of(i * R + SUB, SUB), R), :] = take(0, rows) + take(half, rows) * spread(enter)

        state[m, :SUB, :] = shift_down(state[m, L:, :])

    if linked:
        net.drain()
        gather.done()

    @pl.loop(0, parts)
    def _(m):
        for cols in column_halves:
            mixed[:, cols] += dot(state[m, SUB:, :].astype(bf16), wo[m, :, cols])

    @pl.loop(0, L // R)
    def _(i):
        rows = pl.ds(pl.multiple_of(i * R, R), R)
        x = mixed[rows, :]
        r = lax.rsqrt(jnp.mean(x * x, axis=-1, keepdims=True) + norm_eps)
        n2[rows, :] = (x * r * gain_two).astype(bf16)
        acc_a[rows, :] = x
        acc_b[rows, :] = jnp.zeros_like(x)

    n2t[...] = n2[...].T

    @pl.loop(0, parts)
    def _(turn):
        m = of_turn(turn)
        for first in range(0, fm, fm // 2):
            units_of = slice(first, first + fm // 2)
            up = dot(n2[...], wu[m, :, units_of])
            da = dot(cot[...], wd[m, units_of, :], True)
            cdf, xpdf = gelu_terms(up)
            act[:, units_of] = (up * cdf).astype(bf16)
            dup[:, units_of] = (da * (cdf + xpdf)).astype(bf16)
            if linked and first == 0:
                for k in (2, 3):

                    @pl.when(turn == k)
                    def _():
                        reduce.plane(UPDOWN, k - 1)

        for cols in column_halves:
            acc_a[:, cols] += dot(act[...], wd[m, :, cols])
        for cols in column_halves:
            acc_b[:, cols] += dot(dup[...], wu[m, cols, :], True)
        for c in range(0, fm, fm // 2):
            part = slice(c, c + fm // 2)
            stack(m, 0, fm // BLK, c // BLK, dot(n2t[...], dup[:, part]))
        for c in range(0, fm, fm // 2):
            part = slice(c, c + fm // 2)
            stack_turned(m, units[UPDOWN][1] // 2 + c // BLK * (D // BLK), dot(cott[...], act[:, part]))
        if linked:
            for k in (1, 2, 3):

                @pl.when(turn == k)
                def _():
                    if k == 1:
                        gather.all_done()
                    reduce.chip(UPDOWN, k)

    permute_out(acc_a, n1)
    push_out = pltpu.make_async_copy(n1, block_out, local.at[0])
    push_out.start()

    if linked:
        reduce.model(UPDOWN, 1)
        reduce.turn(UPDOWN, 2)
        reduce.plane(UPDOWN, 3)

    gain_sum_two = jnp.zeros((1, D), f32)

    def back_two(i, total):
        rows = pl.ds(pl.multiple_of(i * R, R), R)
        x = mixed[rows, :]
        r = lax.rsqrt(jnp.mean(x * x, axis=-1, keepdims=True) + norm_eps)
        dn = acc_b[rows, :]
        q = dn * gain_two
        d = cot[rows, :].astype(f32) + r * q - r * r * r * x * jnp.mean(q * x, axis=-1, keepdims=True)
        mixed[rows, :] = d
        dml[rows, :] = d.astype(bf16)
        acc_b[rows, :] = jnp.zeros_like(d)
        return total + jnp.sum(dn * x * r, axis=0, keepdims=True)

    gain_sum_two = lax.fori_loop(0, L // R, back_two, gain_sum_two)
    dmlt[...] = dml[...].T
    fetch_tok = pltpu.make_async_copy(tokens, cot, local.at[1])
    fetch_tok.start()

    @pl.loop(0, parts)
    def _(m):
        stack_turned(m, units[OUT][0], dot(dmlt[...], state[m, SUB:, :].astype(bf16)))

    if linked:
        for i in (3, 2, 1):
            reduce.chip(OUT, i)

    @pl.loop(0, parts)
    def _(back_turn):
        turn = parts - 1 - back_turn
        m = of_turn(turn)
        put(0, slice(None), dot(dml[...], wo[m], True))

        @pl.loop(0, L // R)
        def _(i):
            rows = pl.ds(pl.multiple_of(i * R, R), R)
            f = forget[m, rows, :]
            kept[rows, :] = f * recip(f + admit[m, rows, :])

        def step(k, carry):
            u, p, keep_next = carry
            j = J - 1 - k
            rows = pl.ds(pl.multiple_of(j * SUB, SUB), SUB)
            u = take(0, rows) + keep_next * u
            p = keep_next * p
            put(0, rows, u)
            put(half, rows, p)
            return u, p, kept[rows, :]

        u, p, keep_first = lax.fori_loop(0, J, step, (fills[0], fills[1], fills[1]), unroll=16)
        enter = fills[0]
        for _ in range(SUB - 1):
            enter = shift_up(keep_first * (u + p * enter))

        if linked:

            @pl.when(turn == 3)
            def _():
                reduce.turn(UPDOWN, 3)
                reduce.model(UPDOWN, 2)
                for i in (3, 2, 1):
                    reduce.plane(OUT, i)

            @pl.when(turn == 2)
            def _():
                reduce.model(UPDOWN, 3)
                for i in (3, 2):
                    reduce.turn(OUT, i)
                reduce.plane(GATE, 3)

            @pl.when(turn == 1)
            def _():
                for i in (1, 3, 2):
                    reduce.model(OUT, i)
                reduce.turn(GATE, 3)
                reduce.plane(GATE, 2)

            @pl.when(turn == 0)
            def _():
                reduce.plane(GATE, 1)
                reduce.model(GATE, 3)
                reduce.turn(GATE, 2)

        @pl.loop(0, L // R)
        def _(i):
            rows = pl.ds(pl.multiple_of(i * R, R), R)
            carried = take(0, rows) + take(half, rows) * spread(enter)
            f = forget[m, rows, :]
            a = admit[m, rows, :]
            adm = a * recip(f + a)
            g = carried * (state[m, rows, :] - cand[m, rows, :]) * (kept[rows, :] * adm)
            dpre[rows, :hm] = (g * (1.0 - f)).astype(bf16)
            dpre[rows, hm : 2 * hm] = (g * (a - 1.0)).astype(bf16)
            dpre[rows, 2 * hm :] = (carried * adm).astype(bf16)

        for k in range(3):
            stack(m, units[GATE][0], 3 * hm // BLK, k * hm // BLK, dot(n1t[...], dpre[:, k * hm : (k + 1) * hm]))
        if linked:
            for k in (3, 2, 1):

                @pl.when(turn == k)
                def _():
                    reduce.chip(GATE, k)

        for cols in column_halves:
            acc_b[:, cols] += dot(dpre[...], wg[m, cols, :], True)

    if linked:
        reduce.model(GATE, 1)
        reduce.model(GATE, 2)
        reduce.own(UPDOWN)
        reduce.own(OUT)

    fetch_tok.wait()
    permute_in(cot, cot)

    def back_one(i, total):
        rows = pl.ds(pl.multiple_of(i * R, R), R)
        x = cot[rows, :].astype(f32)
        r = lax.rsqrt(jnp.mean(x * x, axis=-1, keepdims=True) + norm_eps)
        dn = acc_b[rows, :]
        q = dn * gain_one
        mixed[rows, :] += r * q - r * r * r * x * jnp.mean(q * x, axis=-1, keepdims=True)
        return total + jnp.sum(dn * x * r, axis=0, keepdims=True)

    gain_sum_one = lax.fori_loop(0, L // R, back_one, jnp.zeros((1, D), f32))

    place = lax.broadcasted_iota(jnp.int32, (SUB, hm), 0).astype(f32) * float(J)
    if linked:
        first = ((gather.me * parts + gather.m) * L + 1).astype(f32)
        token_total = float(L * parts * lax.axis_size("dp"))
    else:
        first = base[0]
        token_total = base[1]
    forget_sum = jnp.sum(tally[1] + tally[0] * (place + first), axis=0, keepdims=True) / token_total
    small[...] = jnp.zeros_like(small)
    small[0:1, :] = gain_sum_one
    small[1:2, :] = gain_sum_two
    small[2:3, :hm] = forget_sum
    if linked:
        flat = units[UPDOWN][1] // 2, units[GATE][0]
        count = owned.shape[0]
        flags = []
        for k in range(count):
            spot = slot_place[gather.me * count + k]
            flags.append(jnp.where((spot >= flat[0]) & (spot < flat[1]), 1.0, 0.0).astype(f32))

    if linked:
        tiny = SmallSum(net, gather, small, sum_a, sum_b, sum_c)
        tiny.send(0)
        reduce.own(GATE)
        reduce.slots_chip(slots, slot_place, pair)
        tiny.add(0)
        tiny.send(1)
        reduce.slots_plane(slots, pair, far)

    permute_out(mixed, acc_a)
    push_grad = pltpu.make_async_copy(acc_a, input_grad, local.at[2])
    push_grad.start()

    if linked:
        tiny.add(1)
        tiny.send(2)
        reduce.slots_end(slots, pair, far, owned)
        tiny.add(2)
        for k, flag in enumerate(flags):
            small[3 + k // 4 : 4 + k // 4, (k % 4) * BLK : (k % 4 + 1) * BLK] = jnp.full((1, BLK), flag, f32)
        net.drain()
    push_out.wait()
    push_grad.wait()


def compute(tokens, cotangent, gains, weights=None, base=None, master=None, rank=None, slot_place=None):
    linked = weights is None
    parts = lax.axis_size("mp")
    hm, fm = H // parts, FF // parts
    stacked = (parts, D * (4 * hm + 2 * fm) // BLK**2, BLK, BLK)
    sds = jax.ShapeDtypeStruct
    vm, sm, hbm = (pl.BlockSpec(memory_space=k) for k in (pltpu.VMEM, pltpu.SMEM, pl.ANY))
    if linked:
        n = rank.shape[0]
        args = (tokens, cotangent, master, rank, slot_place, gains)
        in_specs = [hbm, hbm, vm, sm, sm, vm]
        middle = sds((n // 8, BLK, BLK), f32)
        extra = [
            pltpu.VMEM((parts, D, 3 * hm), bf16),
            pltpu.VMEM((parts, hm, D), bf16),
            pltpu.VMEM((parts, D, fm), bf16),
            pltpu.VMEM((parts, fm, D), bf16),
            pltpu.VMEM(stacked, bf16),
            pltpu.VMEM((n, BLK, BLK), bf16),
            *[pltpu.VMEM((n, BLK, BLK), bf16) for _ in range(parts - 1)],
            pltpu.VMEM((n // 2, BLK, BLK), bf16),
            pltpu.VMEM((6, n // 16, BLK, BLK), bf16),
            pltpu.VMEM((parts, 8, D), f32),
            pltpu.VMEM((4, 8, D), f32),
            pltpu.VMEM((2, 8, D), f32),
            pltpu.SemaphoreType.DMA((128,)),
            pltpu.SemaphoreType.DMA((128,)),
            pltpu.SemaphoreType.REGULAR,
        ]
        params = dict(collective_id=0, has_side_effects=True)
    else:
        args = (tokens, cotangent, base, *weights, gains)
        in_specs = [hbm, hbm, sm] + [vm] * 5
        middle = sds(stacked, bf16)
        extra = []
        params = {}
    return pl.pallas_call(
        functools.partial(compute_kernel, linked),
        out_shape=(sds((L, D), bf16), sds((L, D), f32), middle, sds((8, D), f32)),
        in_specs=in_specs,
        out_specs=[hbm, hbm, vm, vm],
        scratch_shapes=extra
        + [pltpu.VMEM(shape, bf16) for shape in ((L, D), (D, L)) * 3]
        + [pltpu.VMEM((parts, L, hm), f32)] * 3
        + [pltpu.VMEM((parts, L + SUB, hm), f32)]
        + [pltpu.VMEM((2 * hm // BLK, L, BLK), f32)]
        + [pltpu.VMEM((L, D), f32)] * 3
        + [
            pltpu.VMEM((L, 2 * fm), bf16),
            pltpu.VMEM((L, hm), f32),
            pltpu.VMEM((2, SUB, hm), f32),
            pltpu.VMEM((2, SUB, hm), f32),
            pltpu.SemaphoreType.DMA((3,)),
        ],
        compiler_params=pltpu.CompilerParams(vmem_limit_bytes=64 * 2**20 - 2**16, **params),
        name="block",
    )(*args)


def adam_update(first_old, second_old, gradient):
    first_new = beta_one * first_old + (1.0 - beta_one) * gradient
    second_new = beta_two * second_old + (1.0 - beta_two) * gradient * gradient
    first_hat = first_new / (1.0 - beta_one**STEP)
    second_hat = second_new / (1.0 - beta_two**STEP)
    return (first_new, second_new, first_hat / (jnp.sqrt(second_hat) + adam_eps))


def fine_dot(a, b, trans_b=False):
    a_high, b_high = a.astype(bf16), b.astype(bf16)
    a_low, b_low = (a - a_high.astype(f32)).astype(bf16), (b - b_high.astype(f32)).astype(bf16)
    return dot(a_high, b_high, trans_b) + (dot(a_high, b_low, trans_b) + dot(a_low, b_high, trans_b))


def update_kernel(token_total, passed, sums, gains, gain_moment_one, gain_moment_two, *refs):
    sources, refs = refs[:6], refs[6:]
    given, refs = refs[:passed], refs[passed:]
    results, refs = refs[:4], refs[4:]
    gain_first, gain_second, gains_new, forget_mean = refs[:4]
    copied, refs = refs[4 : 4 + passed], refs[4 + passed :]
    held, made, made_low, sem_in, sem_out, sem_pass = refs[:6]
    passage = refs[6:]
    count = held.shape[1]
    step = max(count // 2, 1)
    groups = [slice(first, first + step) for first in range(0, count, step)]
    enter = [pltpu.make_async_copy(src, via, sem_pass.at[0, k]) for k, (src, via) in enumerate(zip(given, passage))]
    leave = [pltpu.make_async_copy(via, dst, sem_pass.at[1, k]) for k, (via, dst) in enumerate(zip(passage, copied))]
    fetch = [
        [pltpu.make_async_copy(src.at[group], held.at[k, group], sem_in.at[g, k]) for k, src in enumerate(sources)]
        for g, group in enumerate(groups)
    ]
    for copy in fetch[0]:
        copy.start()
    for copy in enter:
        copy.start()
    for row in fetch[1:]:
        for copy in row:
            copy.start()
    first, second, direction = adam_update(gain_moment_one[...], gain_moment_two[...], sums[0:2, :])
    gain_first[...] = first
    gain_second[...] = second
    gains_new[...] = gains[...] - gain_rate * direction
    forget_mean[...] = jnp.sum(sums[2:3, :], axis=1, keepdims=True) * (1.0 / (H * (token_total + 1) / 2.0))
    push = []
    for g, group in enumerate(groups):
        blocks = range(group.start, group.stop)
        for copy in fetch[g]:
            copy.wait()
        if g == len(groups) - 1:
            for come, go in zip(enter, leave):
                come.wait()
                go.start()
        grads = []
        for s in blocks:
            grad = held[0, s]
            flag = sums[3 + s // 4 : 4 + s // 4, (s % 4) * BLK : (s % 4 + 1) * BLK]
            grads.append(jnp.where(flag > 0.5, grad.T, grad))
        values = [fine_dot(held[1, s].T, grad) for s, grad in zip(blocks, grads)]
        values = [fine_dot(value, held[2, s]) for s, value in zip(blocks, values)]
        for k, s in enumerate(blocks):
            first, second, values[k] = adam_update(held[3, s], held[4, s], values[k])
            made[0, s] = first
            made[1, s] = second
        values = [fine_dot(held[1, s], value) for s, value in zip(blocks, values)]
        values = [fine_dot(value, held[2, s], True) for s, value in zip(blocks, values)]
        for s, value in zip(blocks, values):
            fresh = held[5, s] - learn_rate * (value + weight_decay * held[5, s])
            made[2, s] = fresh
            made_low[s] = fresh.astype(bf16)
        for k, dst in enumerate(results):
            src = made.at[k, group] if k < 3 else made_low.at[group]
            copy = pltpu.make_async_copy(src, dst.at[group], sem_out.at[g, k])
            copy.start()
            push.append(copy)
    for copy in push + leave:
        copy.wait()


def update(token_total, small, large, passed):
    sds = jax.ShapeDtypeStruct
    blocks, gain = large[0].shape, small[1].shape
    vm, hbm = pl.BlockSpec(memory_space=pltpu.VMEM), pl.BlockSpec(memory_space=pl.ANY)
    return pl.pallas_call(
        functools.partial(update_kernel, token_total, len(passed)),
        out_shape=[sds(blocks, f32)] * 3
        + [sds(blocks, bf16)]
        + [sds(gain, f32)] * 3
        + [sds((1, 1), f32)]
        + [sds(v.shape, v.dtype) for v in passed],
        in_specs=[vm] * 4 + [hbm] * (len(large) + len(passed)),
        out_specs=[hbm] * 4 + [vm] * 4 + [hbm] * len(passed),
        scratch_shapes=[
            pltpu.VMEM((6, *blocks), f32),
            pltpu.VMEM((3, *blocks), f32),
            pltpu.VMEM(blocks, bf16),
            pltpu.SemaphoreType.DMA((2, 6)),
            pltpu.SemaphoreType.DMA((2, 4)),
            pltpu.SemaphoreType.DMA((2, len(passed))),
        ]
        + [pltpu.VMEM(v.shape, v.dtype) for v in passed],
        compiler_params=pltpu.CompilerParams(vmem_limit_bytes=56 * 2**20),
        name="update",
    )(*small, *large, *passed)


def on_device(
    tokens,
    cotangent,
    master,
    moment_one,
    moment_two,
    basis_left,
    basis_right,
    owner,
    gains,
    gain_moment_one,
    gain_moment_two,
):
    parts = lax.axis_size("mp")
    data_parts = lax.axis_size("dp")
    hm, fm = H // parts, FF // parts
    token_total = L * data_parts * parts
    row_tiles, cols, lows = D // BLK, (3 * hm + fm) // BLK, (hm + fm) // BLK
    number = jnp.arange(owner.shape[0], dtype=jnp.int32)
    ahead = (owner[None, :] < owner[:, None]) | ((owner[None, :] == owner[:, None]) & (number[None, :] < number[:, None]))
    block_rank = jnp.sum(ahead.astype(jnp.int32), axis=1)
    _, table = stack_places(hm, fm)
    table = jnp.asarray(table, jnp.int32)
    slot_place = jnp.sum(jnp.where(block_rank[None, :] == number[:, None], table[None, :], 0), axis=1)
    if data_parts == 8 and parts == 4:
        block_out, input_grad, owned, sums = compute(
            tokens, cotangent, gains, master=master[0], rank=block_rank, slot_place=slot_place
        )
    else:
        stored = lax.all_gather(master.astype(bf16), "dp", axis=1, tiled=True)
        stored = lax.all_gather(stored, "mp", axis=0, tiled=True)
        stack = stored[:, block_rank]
        upper = stack[:, : row_tiles * cols].reshape(parts, row_tiles, cols, BLK, BLK)
        upper = upper.transpose(0, 1, 3, 2, 4).reshape(parts, D, cols * BLK)
        lower = stack[:, row_tiles * cols :].reshape(parts, lows, row_tiles, BLK, BLK)
        lower = lower.transpose(0, 1, 3, 2, 4).reshape(parts, lows * BLK, D)
        weights = (upper[:, :, : 3 * hm], lower[:, :hm], upper[:, :, 3 * hm :], lower[:, hm:])
        first = ((lax.axis_index("dp") * parts + lax.axis_index("mp")) * L + 1).astype(f32)
        base = jnp.stack([first, jnp.asarray(token_total, f32)])
        block_out, input_grad, grads, sums = compute(tokens, cotangent, gains, weights=weights, base=base)
        owned = lax.psum_scatter(grads[:, slot_place].astype(f32), "dp", scatter_dimension=1, tiled=True)
        owned = lax.psum_scatter(owned, "mp", scatter_dimension=0, tiled=True)[0]
        sums = lax.psum(sums, ("dp", "mp"))
        count = master.shape[1]
        mine = lax.dynamic_slice_in_dim(slot_place, lax.axis_index("dp") * count, count)
        units, _ = stack_places(hm, fm)
        flags = ((mine >= units[UPDOWN][1] // 2) & (mine < units[GATE][0])).astype(f32)
        flags = jnp.pad(jnp.repeat(flags, BLK), (0, (8 - count) * BLK)).reshape(2, 4 * BLK)
        sums = jnp.concatenate([sums[:3], flags, sums[5:]])
    outs = update(
        token_total,
        (sums, gains, gain_moment_one, gain_moment_two),
        (owned, basis_left[0], basis_right[0], moment_one[0], moment_two[0], master[0]),
        (block_out, input_grad),
    )
    first_new, second_new, master_new, master_low, gain_first, gain_second, gains_new, forget_mean = outs[:8]
    block_out, input_grad = outs[8:]
    return (
        block_out,
        input_grad,
        first_new[None],
        second_new[None],
        master_new[None],
        master_low[None],
        gain_first,
        gain_second,
        gains_new,
        forget_mean[0, 0],
    )


def solution(mesh):
    rows, blocks = P(("dp", "mp"), None), P("mp", "dp", None, None)
    return jax.shard_map(
        on_device,
        mesh=mesh,
        in_specs=(rows, rows, blocks, blocks, blocks, blocks, blocks, P(), P(), P(), P()),
        out_specs=(rows, rows, blocks, blocks, blocks, blocks, P(), P(), P(), P()),
        check_vma=False,
    )
```

profile of v0, /device:TPU:0, one launch (start us, length us, event | category | flops | bytes accessed | tf_op | source)
XLA Modules:
  0.0 135.7 jit_solution(10847530360256808298)
XLA Ops:
  0.6 0.9 convert_reduce_fusion.refs_3_
  1.6 0.0 copy-start
  1.6 0.5 copy-done
  2.1 1.3 select_reduce_fusion.refs_4_
  3.4 125.7 %block.1 = (bf16[1024,512]{1,0:T(8,128)(2,1)}, f32[1024,512]{1,0:T(8,128)}, f32[8,128,128]{2,1,0:T(8,128)}, f32[8,512]{1,0:T(8,128)}) custom-call(bf16[1024,512]{1,0:T(8,128)(2,1)} %refs_0_.1, bf16[1024,512]{1,0:T(8,128)(2,1)} %refs_1_.1, f32[8,128,128]{2,1,0:T(8,128)} %bitcast.10, s32[64]{0:T(128)} %copy-done, s32[64]{0:T(128)} %select_reduce_fusion.refs_4_, ...), custom_call_target="tpu_custom_call" | custom-call | tf_op jit(solution)/shard_map/block/pallas_call | solution.py:919
  129.1 6.4 %update.1 = (f32[8,128,128]{2,1,0:T(8,128)}, f32[8,128,128]{2,1,0:T(8,128)}, f32[8,128,128]{2,1,0:T(8,128)}, bf16[8,128,128]{2,1,0:T(8,128)(2,1)}, f32[2,512]{1,...) custom-call(f32[8,512]{1,0:T(8,128)} %get-tuple-element.24.sums, ...), custom_call_target="tpu_custom_call" | custom-call | tf_op jit(solution)/shard_map/update/pallas_call | solution.py:1024
Async XLA Ops:
  1.6 0.5 copy-start
where the time goes:
time: 136 us
  Pallas kernels  132 us (97%)
  other arithmetic  2.19 us (2%)
    pallas_call x1, Pallas kernels, compute(): pl.pallas_call(functools.partial(compute_kernel, linked), out_shape=(sds(...  126 us
    pallas_call x1, Pallas kernels, update(): pl.pallas_call(functools.partial(update_kernel, token_total, len(passed))...  6.41 us

commit v1 on v0

--- a/solution.py
+++ b/solution.py
@@ -258,7 +258,6 @@
         self.net, self.g, self.grads, self.units, self.pool = net, gather, grads, units, pool
         self.half = grads.shape[1] // 2
         self.eighth = grads.shape[1] // 8
-        self.copies = {}
 
     def place(self, e):
         return (e % 2) * 4 + e // 2
@@ -292,15 +291,40 @@
         base, total = self.units[unit]
         return self.grads.at[self.g.order[i], pl.ds(base + self.place(e) * (total // 8) + first, count)]
 
-    def send(self, unit, i, e, part, slot, to):
+    def over(self, unit, i, slot, part):
+        x, y, z = self.g.plane
+        e = (z, x, y)[slot]
+        to = (x if part == self.parts(unit, i)[0] else y, x, y)[slot]
+        return self.net.copy(
+            lambda: (self.share(unit, i, e, *part), self.spot(unit, i, slot, *part), (to, self.g.m)),
+            ("over", unit, i, slot, part),
+        )
+
+    def send(self, unit, i, slot, part):
         if part[1]:
-            self.copies[1, unit, i, slot, part] = self.net.start(
-                lambda: (self.share(unit, i, e, *part), self.spot(unit, i, slot, *part), (to, self.g.m))
-            )
+            self.over(unit, i, slot, part).start()
 
     def take(self, unit, i, slot, part):
-        self.copies[1, unit, i, slot, part].wait_recv()
+        self.over(unit, i, slot, part).wait_recv()
         return self.spot(unit, i, slot, *part)[...].astype(f32)
+
+    def model_copy(self, unit, i):
+        n = self.units[unit][1] // 8
+        return self.net.copy(
+            lambda: (self.share(unit, i, self.g.me, 0, n), self.spot(unit, i, 3, 0, n), (self.g.me, self.g.order[i])),
+            ("model", unit, i),
+        )
+
+    def aside(self, unit):
+        part = (0, self.units[unit][1] // 8)
+        return self.net.copy(
+            lambda: (
+                self.share(unit, 1, self.g.plane[2], *part),
+                self.spot(unit, 1, 0, *part),
+                (self.g.me, self.g.order[1]),
+            ),
+            ("aside", unit),
+        )
 
     def plane(self, unit, i):
         g, (first, count) = self.g, self.units[unit]
@@ -316,27 +340,25 @@
 
         if i == 1:
             (whole,) = self.parts(unit, i)
-            self.send(unit, i, x, whole, 1, x)
-            self.send(unit, i, y, whole, 2, y)
-            self.copies[3, unit] = self.net.start(
-                lambda: (self.share(unit, i, z, *whole), self.spot(unit, i, 0, *whole), (g.me, g.order[i]))
-            )
+            self.send(unit, i, 1, whole)
+            self.send(unit, i, 2, whole)
+            self.aside(unit).start()
             return
         one, two = self.parts(unit, i)
-        self.send(unit, i, z, one, 0, x)
-        self.send(unit, i, z, two, 0, y)
-        self.send(unit, i, x, one, 1, x)
-        self.send(unit, i, y, two, 2, y)
+        self.send(unit, i, 0, one)
+        self.send(unit, i, 0, two)
+        self.send(unit, i, 1, one)
+        self.send(unit, i, 2, two)
 
     def turn(self, unit, i):
         if i == 1:
             return
-        x, y, z = self.g.plane
+        x, y, _ = self.g.plane
         for part, slot, e in zip(self.parts(unit, i), (2, 1), (y, x)):
             if part[1]:
                 ref = self.share(unit, i, e, *part)
                 ref[...] = (ref[...].astype(f32) + self.take(unit, i, 0, part)).astype(bf16)
-                self.send(unit, i, e, part, slot, e)
+                self.send(unit, i, slot, part)
 
     def model(self, unit, i):
         g, (first, count) = self.g, self.units[unit]
@@ -346,9 +368,7 @@
                 ref = self.share(unit, i, g.me, *part)
                 total = ref[...].astype(f32) + self.take(unit, i, 1, part) + self.take(unit, i, 2, part)
                 ref[...] = total.astype(bf16)
-        self.copies[2, unit, i] = self.net.start(
-            lambda: (self.share(unit, i, g.me, 0, n), self.spot(unit, i, 3, 0, n), (g.me, g.order[i]))
-        )
+        self.model_copy(unit, i).start()
 
     def own(self, unit):
         g, (first, count) = self.g, self.units[unit]
@@ -356,10 +376,10 @@
         rows = pl.ds(first + self.place(g.me) * n, n)
         total = self.grads[g.m, rows].astype(f32)
         for i in (1, 2, 3):
-            self.copies[2, unit, i].wait_recv()
+            self.model_copy(unit, i).wait_recv()
             total += self.pool[i - 1][pl.ds(self.half + 3 * self.eighth + first // 8, n)].astype(f32)
         self.grads[g.m, rows] = total.astype(bf16)
-        self.copies[3, unit].wait_recv()
+        self.aside(unit).wait_recv()
         rows = pl.ds(first + self.place(g.plane[2]) * n, n)
         total = self.grads[g.m, rows].astype(f32) + self.spot(unit, 1, 0, 0, n)[...].astype(f32)
         self.grads[g.m, rows] = total.astype(bf16)
@@ -542,6 +562,7 @@
         gather = Gather(net, master, rank, slots, pool, (wg, wo, wu, wd), free)
         gather.start(0)
         gather.along_start(1)
+        gather.along_start(2)
         reduce = Reduce(net, gather, grads, units, pool)
 
     def of_turn(t):
@@ -566,7 +587,6 @@
 
     if linked:
         gather.forward(0)
-        gather.along_start(2)
         gather.along_start(3)
     fetch_cot.wait()
     permute_in(cot, cot)
@@ -574,6 +594,7 @@
         gather.start(1)
         gather.pair(0)
         gather.across_start()
+        gather.start(2)
     cott[...] = cot[...].T
 
     fills[0] = jnp.zeros((SUB, hm), f32)
@@ -603,10 +624,12 @@
 
                 @pl.when(turn == k)
                 def _():
-                    if k:
-                        gather.forward(k + 1)
-                    if k < 2:
-                        gather.start(k + 2)
+                    if k == 0:
+                        gather.forward(2)
+                    if k == 1:
+                        gather.start(3)
+                    if k == 2:
+                        gather.forward(3)
 
         @pl.loop(0, L // R)
         def _(i):
@@ -673,17 +696,19 @@
             cdf, xpdf = gelu_terms(up)
             act[:, units_of] = (up * cdf).astype(bf16)
             dup[:, units_of] = (da * (cdf + xpdf)).astype(bf16)
-            if linked and first == 0:
-                for k in (2, 3):
-
-                    @pl.when(turn == k)
-                    def _():
-                        reduce.plane(UPDOWN, k - 1)
-
         for cols in column_halves:
             acc_a[:, cols] += dot(act[...], wd[m, :, cols])
         for cols in column_halves:
             acc_b[:, cols] += dot(dup[...], wu[m, cols, :], True)
+        if linked:
+            for k in (2, 3):
+
+                @pl.when(turn == k)
+                def _():
+                    reduce.plane(UPDOWN, k - 1)
+                    if k == 3:
+                        reduce.model(UPDOWN, 1)
+
         for c in range(0, fm, fm // 2):
             part = slice(c, c + fm // 2)
             stack(m, 0, fm // BLK, c // BLK, dot(n2t[...], dup[:, part]))
@@ -704,8 +729,6 @@
     push_out.start()
 
     if linked:
-        reduce.model(UPDOWN, 1)
-        reduce.turn(UPDOWN, 2)
         reduce.plane(UPDOWN, 3)
 
     gain_sum_two = jnp.zeros((1, D), f32)
@@ -723,6 +746,8 @@
         return total + jnp.sum(dn * x * r, axis=0, keepdims=True)
 
     gain_sum_two = lax.fori_loop(0, L // R, back_two, gain_sum_two)
+    if linked:
+        reduce.turn(UPDOWN, 2)
     dmlt[...] = dml[...].T
     fetch_tok = pltpu.make_async_copy(tokens, cot, local.at[1])
     fetch_tok.start()
@@ -766,30 +791,12 @@
 
             @pl.when(turn == 3)
             def _():
-                reduce.turn(UPDOWN, 3)
-                reduce.model(UPDOWN, 2)
                 for i in (3, 2, 1):
                     reduce.plane(OUT, i)
-
-            @pl.when(turn == 2)
-            def _():
-                reduce.model(UPDOWN, 3)
-                for i in (3, 2):
-                    reduce.turn(OUT, i)
-                reduce.plane(GATE, 3)
-
-            @pl.when(turn == 1)
-            def _():
-                for i in (1, 3, 2):
-                    reduce.model(OUT, i)
-                reduce.turn(GATE, 3)
-                reduce.plane(GATE, 2)
 
             @pl.when(turn == 0)
             def _():
                 reduce.plane(GATE, 1)
-                reduce.model(GATE, 3)
-                reduce.turn(GATE, 2)
 
         @pl.loop(0, L // R)
         def _(i):
@@ -803,6 +810,31 @@
             dpre[rows, hm : 2 * hm] = (g * (a - 1.0)).astype(bf16)
             dpre[rows, 2 * hm :] = (carried * adm).astype(bf16)
 
+        if linked:
+
+            @pl.when(turn == 3)
+            def _():
+                reduce.turn(UPDOWN, 3)
+                reduce.model(UPDOWN, 2)
+
+            @pl.when(turn == 2)
+            def _():
+                reduce.plane(GATE, 3)
+                for i in (3, 2):
+                    reduce.turn(OUT, i)
+                reduce.model(UPDOWN, 3)
+
+            @pl.when(turn == 1)
+            def _():
+                reduce.plane(GATE, 2)
+                for i in (1, 3, 2):
+                    reduce.model(OUT, i)
+
+            @pl.when(turn == 0)
+            def _():
+                reduce.turn(GATE, 2)
+                reduce.model(GATE, 3)
+
         for k in range(3):
             stack(m, units[GATE][0], 3 * hm // BLK, k * hm // BLK, dot(n1t[...], dpre[:, k * hm : (k + 1) * hm]))
         if linked:
@@ -811,18 +843,21 @@
                 @pl.when(turn == k)
                 def _():
                     reduce.chip(GATE, k)
+                    if k == 1:
+                        reduce.turn(GATE, 3)
 
         for cols in column_halves:
             acc_b[:, cols] += dot(dpre[...], wg[m, cols, :], True)
 
     if linked:
+        reduce.own(UPDOWN)
+        reduce.own(OUT)
+
+    fetch_tok.wait()
+    permute_in(cot, cot)
+    if linked:
         reduce.model(GATE, 1)
         reduce.model(GATE, 2)
-        reduce.own(UPDOWN)
-        reduce.own(OUT)
-
-    fetch_tok.wait()
-    permute_in(cot, cot)
 
     def back_one(i, total):
         rows = pl.ds(pl.multiple_of(i * R, R), R)

time: 136 us -> 133 us (0.978)
  Pallas kernels: 132 us -> 129 us
    pallas_call x1, Pallas kernels: 126 us -> 123 us  [compute(): pl.pallas_call(functools.partial(compute_kernel, linked), out_shape=(sds(...]
where the time goes in v1:
time: 133 us
  Pallas kernels  129 us (97%)
  other arithmetic  2.19 us (2%)
    pallas_call x1, Pallas kernels, compute(): pl.pallas_call(functools.partial(compute_kernel, linked), out_shape=(sds(...  123 us
    pallas_call x1, Pallas kernels, update(): pl.pallas_call(functools.partial(update_kernel, token_total, len(passed))...  6.42 us

profile of v1, /device:TPU:0, one launch (start us, length us, event | category | flops | bytes accessed | tf_op | source)
XLA Modules:
  0.0 132.5 jit_solution(808706770008710060)
XLA Ops:
  0.6 0.9 convert_reduce_fusion.refs_3_
  1.6 0.0 copy-start
  1.6 0.5 copy-done
  2.1 1.3 select_reduce_fusion.refs_4_
  3.4 122.6 %block.1 = (bf16[1024,512]{1,0:T(8,128)(2,1)}, f32[1024,512]{1,0:T(8,128)}, f32[8,128,128]{2,1,0:T(8,128)}, f32[8,512]{1,0:T(8,128)}) custom-call(bf16[1024,512]{1,0:T(8,128)(2,1)} %refs_0_.1, bf16[1024,512]{1,0:T(8,128)(2,1)} %refs_1_.1, f32[8,128,128]{2,1,0:T(8,128)} %bitcast.10, s32[64]{0:T(128)} %copy-done, s32[64]{0:T(128)} %select_reduce_fusion.refs_4_, ...), custom_call_target="tpu_custom_call" | custom-call | tf_op jit(solution)/shard_map/block/pallas_call | solution.py:954
  126.0 6.4 %update.1 = (f32[8,128,128]{2,1,0:T(8,128)}, f32[8,128,128]{2,1,0:T(8,128)}, f32[8,128,128]{2,1,0:T(8,128)}, bf16[8,128,128]{2,1,0:T(8,128)(2,1)}, f32[2,512]{1,...) custom-call(f32[8,512]{1,0:T(8,128)} %get-tuple-element.24.sums, ...), custom_call_target="tpu_custom_call" | custom-call | tf_op jit(solution)/shard_map/update/pallas_call | solution.py:1059
Async XLA Ops:
  1.6 0.5 copy-start

commit v2 on v1

--- a/solution.py
+++ b/solution.py
@@ -127,8 +127,8 @@
 
 
 class Gather:
-    def __init__(self, net, master, rank, slots, pool, weights, free):
-        self.net, self.weights, self.rank, self.free = net, weights, rank, free
+    def __init__(self, net, fetch, master, slots, pool, weights, free):
+        self.net, self.weights, self.free = net, weights, free
         self.held = [slots, *pool]
         d, m = lax.axis_index("dp"), lax.axis_index("mp")
         core, col, row = d % 2, (d // 2) % 2, d // 4
@@ -141,6 +141,7 @@
         for device in self.peers:
             pl.semaphore_signal(barrier, inc=1, device_id=device, device_id_type=MESH)
         self.n = master.shape[0]
+        fetch.wait()
         for s in range(self.n):
             slots[d * self.n + s] = master[s].astype(bf16)
         pl.semaphore_wait(barrier, len(self.peers))
@@ -209,7 +210,7 @@
         for copy in self.inside(i):
             copy.wait_recv()
 
-    def place(self, i):
+    def place(self, i, rank):
         wg, wo, wu, wd = self.weights
         row_tiles, gates = D // BLK, wg.shape[2] // BLK
         cols, outs = gates + wu.shape[2] // BLK, wo.shape[1] // BLK
@@ -222,7 +223,7 @@
                 r, c = (b - row_tiles * cols) // row_tiles, (b - row_tiles * cols) % row_tiles
                 ref = wo if r < outs else wd
                 r -= 0 if r < outs else outs
-            block = self.held[i][self.rank[b]]
+            block = self.held[i][rank[0, b]]
             ref[self.order[i], r * BLK : (r + 1) * BLK, c * BLK : (c + 1) * BLK] = block
 
     def done(self):
@@ -387,7 +388,7 @@
     def into_slots(self, out, slot_place, e):
         n = self.eighth
         for k in range(n):
-            out[self.place(e) * n + k] = self.grads[self.g.m, slot_place[e * n + k]]
+            out[self.place(e) * n + k] = self.grads[self.g.m, slot_place[0, e * n + k]]
 
     def slots_chip(self, out, slot_place, pair):
         g, n = self.g, self.eighth
@@ -485,12 +486,35 @@
         self.values[...] = total
 
 
+def number_blocks(owner, table, vector, rank, slot_place, sem):
+    lane = lax.broadcasted_iota(jnp.int32, vector.shape, 1)
+    count = owner.shape[0]
+    owners = jnp.zeros_like(lane)
+    for b in range(count):
+        owners = jnp.where(lane == b, owner[b], owners)
+    ranks = jnp.zeros_like(lane)
+    for b in range(count):
+        ahead = (owner[b] < owners) | ((owner[b] == owners) & (lane > b))
+        ranks += jnp.where(ahead, 1, 0)
+    vector[...] = ranks
+    copy = pltpu.make_async_copy(vector, rank, sem)
+    copy.start()
+    copy.wait()
+    places = jnp.zeros_like(lane)
+    for b in range(count):
+        places = jnp.where(lane == rank[0, b], table[b], places)
+    vector[...] = places
+    copy = pltpu.make_async_copy(vector, slot_place, sem)
+    copy.start()
+    copy.wait()
+
+
 def compute_kernel(linked, *refs):
     if linked:
-        tokens, cotangent, master, rank, slot_place, gains = refs[:6]
-        block_out, input_grad, owned, small = refs[6:10]
-        wg, wo, wu, wd, grads, slots, *pool, pair, far, sum_a, sum_b, sum_c, send, recv, free = refs[10:27]
-        scratch = refs[27:]
+        tokens, cotangent, master, owner, gains = refs[:5]
+        block_out, input_grad, owned, small = refs[5:9]
+        wg, wo, wu, wd, grads, slots, *pool, pair, far, sum_a, sum_b, sum_c, vector, rank, slot_place, send, recv, free = refs[9:29]
+        scratch = refs[29:]
     else:
         tokens, cotangent, base, wg, wo, wu, wd, gains = refs[:8]
         block_out, input_grad, grads, small = refs[8:12]
@@ -500,11 +524,14 @@
     parts, _, hm3 = wg.shape
     hm = hm3 // 3
     fm = wu.shape[2]
-    units, _ = stack_places(hm, fm)
+    units, table = stack_places(hm, fm)
     act, dup, dpre = mid.at[:, :fm], mid.at[:, fm:], mid.at[:, : 3 * hm]
     gain_one = gains[0:1, :]
     gain_two = gains[1:2, :]
 
+    if linked:
+        fetch_master = pltpu.make_async_copy(master, owned, local.at[2])
+        fetch_master.start()
     fetch_cot = pltpu.make_async_copy(cotangent, cot, local.at[0])
     fetch_tok = pltpu.make_async_copy(tokens, n1, local.at[1])
     fetch_tok.start()
@@ -559,7 +586,7 @@
 
     if linked:
         net = Exchange(send, recv)
-        gather = Gather(net, master, rank, slots, pool, (wg, wo, wu, wd), free)
+        gather = Gather(net, fetch_master, owned, slots, pool, (wg, wo, wu, wd), free)
         gather.start(0)
         gather.along_start(1)
         gather.along_start(2)
@@ -588,6 +615,7 @@
     if linked:
         gather.forward(0)
         gather.along_start(3)
+        number_blocks(owner, table, vector, rank, slot_place, local.at[2])
     fetch_cot.wait()
     permute_in(cot, cot)
     if linked:
@@ -613,7 +641,7 @@
                     if k:
                         gather.pair(k)
                     gather.ready(k)
-                    gather.place(k)
+                    gather.place(k, rank)
 
         forget[m] = dot(n1[...], wg[m, :, :hm])
         admit[m] = dot(n1[...], wg[m, :, hm : 2 * hm])
@@ -665,15 +693,12 @@
             state[m, pl.ds(pl.multiple_of(i * R + SUB, SUB), R), :] = take(0, rows) + take(half, rows) * spread(enter)
 
         state[m, :SUB, :] = shift_down(state[m, L:, :])
+        for cols in column_halves:
+            mixed[:, cols] += dot(state[m, SUB:, :].astype(bf16), wo[m, :, cols])
 
     if linked:
         net.drain()
         gather.done()
-
-    @pl.loop(0, parts)
-    def _(m):
-        for cols in column_halves:
-            mixed[:, cols] += dot(state[m, SUB:, :].astype(bf16), wo[m, :, cols])
 
     @pl.loop(0, L // R)
     def _(i):
@@ -724,13 +749,6 @@
                         gather.all_done()
                     reduce.chip(UPDOWN, k)
 
-    permute_out(acc_a, n1)
-    push_out = pltpu.make_async_copy(n1, block_out, local.at[0])
-    push_out.start()
-
-    if linked:
-        reduce.plane(UPDOWN, 3)
-
     gain_sum_two = jnp.zeros((1, D), f32)
 
     def back_two(i, total):
@@ -747,7 +765,7 @@
 
     gain_sum_two = lax.fori_loop(0, L // R, back_two, gain_sum_two)
     if linked:
-        reduce.turn(UPDOWN, 2)
+        reduce.plane(UPDOWN, 3)
     dmlt[...] = dml[...].T
     fetch_tok = pltpu.make_async_copy(tokens, cot, local.at[1])
     fetch_tok.start()
@@ -791,6 +809,7 @@
 
             @pl.when(turn == 3)
             def _():
+                reduce.turn(UPDOWN, 2)
                 for i in (3, 2, 1):
                     reduce.plane(OUT, i)
 
@@ -815,7 +834,6 @@
             @pl.when(turn == 3)
             def _():
                 reduce.turn(UPDOWN, 3)
-                reduce.model(UPDOWN, 2)
 
             @pl.when(turn == 2)
             def _():
@@ -823,6 +841,7 @@
                 for i in (3, 2):
                     reduce.turn(OUT, i)
                 reduce.model(UPDOWN, 3)
+                reduce.model(UPDOWN, 2)
 
             @pl.when(turn == 1)
             def _():
@@ -869,6 +888,10 @@
         return total + jnp.sum(dn * x * r, axis=0, keepdims=True)
 
     gain_sum_one = lax.fori_loop(0, L // R, back_one, jnp.zeros((1, D), f32))
+
+    permute_out(acc_a, n1)
+    push_out = pltpu.make_async_copy(n1, block_out, local.at[0])
+    push_out.start()
 
     place = lax.broadcasted_iota(jnp.int32, (SUB, hm), 0).astype(f32) * float(J)
     if linked:
@@ -887,7 +910,7 @@
         count = owned.shape[0]
         flags = []
         for k in range(count):
-            spot = slot_place[gather.me * count + k]
+            spot = slot_place[0, gather.me * count + k]
             flags.append(jnp.where((spot >= flat[0]) & (spot < flat[1]), 1.0, 0.0).astype(f32))
 
     if linked:
@@ -915,7 +938,7 @@
     push_grad.wait()
 
 
-def compute(tokens, cotangent, gains, weights=None, base=None, master=None, rank=None, slot_place=None):
+def compute(tokens, cotangent, gains, weights=None, base=None, master=None, owner=None):
     linked = weights is None
     parts = lax.axis_size("mp")
     hm, fm = H // parts, FF // parts
@@ -923,9 +946,9 @@
     sds = jax.ShapeDtypeStruct
     vm, sm, hbm = (pl.BlockSpec(memory_space=k) for k in (pltpu.VMEM, pltpu.SMEM, pl.ANY))
     if linked:
-        n = rank.shape[0]
-        args = (tokens, cotangent, master, rank, slot_place, gains)
-        in_specs = [hbm, hbm, vm, sm, sm, vm]
+        n = owner.shape[0]
+        args = (tokens, cotangent, master, owner, gains)
+        in_specs = [hbm, hbm, hbm, sm, vm]
         middle = sds((n // 8, BLK, BLK), f32)
         extra = [
             pltpu.VMEM((parts, D, 3 * hm), bf16),
@@ -940,6 +963,9 @@
             pltpu.VMEM((parts, 8, D), f32),
             pltpu.VMEM((4, 8, D), f32),
             pltpu.VMEM((2, 8, D), f32),
+            pltpu.VMEM((8, BLK), jnp.int32),
+            pltpu.SMEM((8, BLK), jnp.int32),
+            pltpu.SMEM((8, BLK), jnp.int32),
             pltpu.SemaphoreType.DMA((128,)),
             pltpu.SemaphoreType.DMA((128,)),
             pltpu.SemaphoreType.REGULAR,
@@ -1097,17 +1123,15 @@
     hm, fm = H // parts, FF // parts
     token_total = L * data_parts * parts
     row_tiles, cols, lows = D // BLK, (3 * hm + fm) // BLK, (hm + fm) // BLK
-    number = jnp.arange(owner.shape[0], dtype=jnp.int32)
-    ahead = (owner[None, :] < owner[:, None]) | ((owner[None, :] == owner[:, None]) & (number[None, :] < number[:, None]))
-    block_rank = jnp.sum(ahead.astype(jnp.int32), axis=1)
-    _, table = stack_places(hm, fm)
-    table = jnp.asarray(table, jnp.int32)
-    slot_place = jnp.sum(jnp.where(block_rank[None, :] == number[:, None], table[None, :], 0), axis=1)
     if data_parts == 8 and parts == 4:
-        block_out, input_grad, owned, sums = compute(
-            tokens, cotangent, gains, master=master[0], rank=block_rank, slot_place=slot_place
-        )
+        block_out, input_grad, owned, sums = compute(tokens, cotangent, gains, master=master[0], owner=owner)
     else:
+        number = jnp.arange(owner.shape[0], dtype=jnp.int32)
+        ahead = (owner[None, :] < owner[:, None]) | ((owner[None, :] == owner[:, None]) & (number[None, :] < number[:, None]))
+        block_rank = jnp.sum(ahead.astype(jnp.int32), axis=1)
+        _, table = stack_places(hm, fm)
+        table = jnp.asarray(table, jnp.int32)
+        slot_place = jnp.sum(jnp.where(block_rank[None, :] == number[:, None], table[None, :], 0), axis=1)
         stored = lax.all_gather(master.astype(bf16), "dp", axis=1, tiled=True)
         stored = lax.all_gather(stored, "mp", axis=0, tiled=True)
         stack = stored[:, block_rank]

time: 133 us -> 132 us (level)
  other arithmetic: 2.19 us -> 0 us
  Pallas kernels: 129 us -> 131 us
    reduce_sum x2 -> x0, other arithmetic: 2.19 us -> none  [the longest x1 1.28 us: on_device(): jnp.sum(jnp.where(block_rank[None, :] == number[:, None], table[None, :],...]
    pallas_call x1, Pallas kernels: 123 us -> 124 us  [compute(): pl.pallas_call(functools.partial(compute_kernel, linked), out_shape=(sds(...]
where the time goes in v2:
time: 132 us; the launch traced here: 131 us
  Pallas kernels  131 us (99%)
    pallas_call x1, Pallas kernels, compute(): pl.pallas_call(functools.partial(compute_kernel, linked), out_shape=(sds(...  124 us
    pallas_call x1, Pallas kernels, update(): pl.pallas_call(functools.partial(update_kernel, token_total, len(passed))...  6.42 us

profile of v2, /device:TPU:0, one launch (start us, length us, event | category | flops | bytes accessed | tf_op | source)
XLA Modules:
  0.0 131.3 jit_solution(7720359017194367044)
XLA Ops:
  0.6 124.1 %block.1 = (bf16[1024,512]{1,0:T(8,128)(2,1)}, f32[1024,512]{1,0:T(8,128)}, f32[8,128,128]{2,1,0:T(8,128)}, f32[8,512]{1,0:T(8,128)}) custom-call(bf16[1024,512]{1,0:T(8,128)(2,1)} %refs_0_.1, bf16[1024,512]{1,0:T(8,128)(2,1)} %refs_1_.1, f32[8,128,128]{2,1,0:T(8,128)} %bitcast.10, s32[64]{0:T(128)} %refs_3_.1, f32[2,512]{1,0:T(2,128)} %gains.1), custom_call_target="tpu_custom_call" | custom-call | tf_op jit(solution)/shard_map/block/pallas_call | solution.py:980
  124.8 6.4 %update.1 = (f32[8,128,128]{2,1,0:T(8,128)}, f32[8,128,128]{2,1,0:T(8,128)}, f32[8,128,128]{2,1,0:T(8,128)}, bf16[8,128,128]{2,1,0:T(8,128)(2,1)}, f32[2,512]{1,...) custom-call(f32[8,512]{1,0:T(8,128)} %get-tuple-element.24.sums, ...), custom_call_target="tpu_custom_call" | custom-call | tf_op jit(solution)/shard_map/update/pallas_call | solution.py:1085

commit v3 on v2

--- a/solution.py
+++ b/solution.py
@@ -27,7 +27,7 @@
 bf16 = jnp.bfloat16
 SUB = 8
 J = L // SUB
-R = 128
+R = 256
 
 
 def dot(a, b, trans_b=False):
@@ -725,15 +725,6 @@
             acc_a[:, cols] += dot(act[...], wd[m, :, cols])
         for cols in column_halves:
             acc_b[:, cols] += dot(dup[...], wu[m, cols, :], True)
-        if linked:
-            for k in (2, 3):
-
-                @pl.when(turn == k)
-                def _():
-                    reduce.plane(UPDOWN, k - 1)
-                    if k == 3:
-                        reduce.model(UPDOWN, 1)
-
         for c in range(0, fm, fm // 2):
             part = slice(c, c + fm // 2)
             stack(m, 0, fm // BLK, c // BLK, dot(n2t[...], dup[:, part]))
@@ -748,6 +739,10 @@
                     if k == 1:
                         gather.all_done()
                     reduce.chip(UPDOWN, k)
+                    if k > 1:
+                        reduce.plane(UPDOWN, k - 1)
+                    if k == 3:
+                        reduce.model(UPDOWN, 1)
 
     gain_sum_two = jnp.zeros((1, D), f32)
 
@@ -778,17 +773,24 @@
         for i in (3, 2, 1):
             reduce.chip(OUT, i)
 
+    def keeps(m, rows):
+        f = forget[m, rows, :]
+        kept[rows, :] = f * recip(f + admit[m, rows, :])
+
+    def state_grads(m):
+        put(0, slice(None), dot(dml[...], wo[m], True))
+
+    state_grads(of_turn(parts - 1))
+
+    @pl.loop(0, L // R)
+    def _(i):
+        keeps(of_turn(parts - 1), pl.ds(pl.multiple_of(i * R, R), R))
+
     @pl.loop(0, parts)
     def _(back_turn):
         turn = parts - 1 - back_turn
         m = of_turn(turn)
-        put(0, slice(None), dot(dml[...], wo[m], True))
-
-        @pl.loop(0, L // R)
-        def _(i):
-            rows = pl.ds(pl.multiple_of(i * R, R), R)
-            f = forget[m, rows, :]
-            kept[rows, :] = f * recip(f + admit[m, rows, :])
+        m_next = of_turn((turn + parts - 1) % parts)
 
         def step(k, carry):
             u, p, keep_next = carry
@@ -828,6 +830,7 @@
             dpre[rows, :hm] = (g * (1.0 - f)).astype(bf16)
             dpre[rows, hm : 2 * hm] = (g * (a - 1.0)).astype(bf16)
             dpre[rows, 2 * hm :] = (carried * adm).astype(bf16)
+            keeps(m_next, rows)
 
         if linked:
 
@@ -856,6 +859,9 @@
 
         for k in range(3):
             stack(m, units[GATE][0], 3 * hm // BLK, k * hm // BLK, dot(n1t[...], dpre[:, k * hm : (k + 1) * hm]))
+        for cols in column_halves:
+            acc_b[:, cols] += dot(dpre[...], wg[m, cols, :], True)
+        state_grads(m_next)
         if linked:
             for k in (3, 2, 1):
 
@@ -864,9 +870,6 @@
                     reduce.chip(GATE, k)
                     if k == 1:
                         reduce.turn(GATE, 3)
-
-        for cols in column_halves:
-            acc_b[:, cols] += dot(dpre[...], wg[m, cols, :], True)
 
     if linked:
         reduce.own(UPDOWN)

time: 132 us -> 130 us (0.985)
  Pallas kernels: 131 us -> 129 us
    pallas_call x1, Pallas kernels: 124 us -> 123 us  [compute(): pl.pallas_call(functools.partial(compute_kernel, linked), out_shape=(sds(...]
where the time goes in v3:
time: 130 us
  Pallas kernels  129 us (99%)
    pallas_call x1, Pallas kernels, compute(): pl.pallas_call(functools.partial(compute_kernel, linked), out_shape=(sds(...  123 us
    pallas_call x1, Pallas kernels, update(): pl.pallas_call(functools.partial(update_kernel, token_total, len(passed))...  6.42 us

profile of v3, /device:TPU:0, one launch (start us, length us, event | category | flops | bytes accessed | tf_op | source)
XLA Modules:
  0.0 129.8 jit_solution(7792355097810887551)
XLA Ops:
  0.6 122.5 %block.1 = (bf16[1024,512]{1,0:T(8,128)(2,1)}, f32[1024,512]{1,0:T(8,128)}, f32[8,128,128]{2,1,0:T(8,128)}, f32[8,512]{1,0:T(8,128)}) custom-call(bf16[1024,512]{1,0:T(8,128)(2,1)} %refs_0_.1, bf16[1024,512]{1,0:T(8,128)(2,1)} %refs_1_.1, f32[8,128,128]{2,1,0:T(8,128)} %bitcast.10, s32[64]{0:T(128)} %refs_3_.1, f32[2,512]{1,0:T(2,128)} %gains.1), custom_call_target="tpu_custom_call" | custom-call | tf_op jit(solution)/shard_map/block/pallas_call | solution.py:983
  123.2 6.4 %update.1 = (f32[8,128,128]{2,1,0:T(8,128)}, f32[8,128,128]{2,1,0:T(8,128)}, f32[8,128,128]{2,1,0:T(8,128)}, bf16[8,128,128]{2,1,0:T(8,128)(2,1)}, f32[2,512]{1,...) custom-call(f32[8,512]{1,0:T(8,128)} %get-tuple-element.24.sums, ...), custom_call_target="tpu_custom_call" | custom-call | tf_op jit(solution)/shard_map/update/pallas_call | solution.py:1088

commit v4 on v3

--- a/solution.py
+++ b/solution.py
@@ -638,7 +638,7 @@
 
                 @pl.when(turn == k)
                 def _():
-                    if k:
+                    if k > 1:
                         gather.pair(k)
                     gather.ready(k)
                     gather.place(k, rank)
@@ -648,16 +648,10 @@
         cand[m] = dot(n1[...], wg[m, :, 2 * hm :])
 
         if linked:
-            for k in range(parts - 1):
-
-                @pl.when(turn == k)
-                def _():
-                    if k == 0:
-                        gather.forward(2)
-                    if k == 1:
-                        gather.start(3)
-                    if k == 2:
-                        gather.forward(3)
+
+            @pl.when(turn == 2)
+            def _():
+                gather.forward(3)
 
         @pl.loop(0, L // R)
         def _(i):
@@ -695,6 +689,13 @@
         state[m, :SUB, :] = shift_down(state[m, L:, :])
         for cols in column_halves:
             mixed[:, cols] += dot(state[m, SUB:, :].astype(bf16), wo[m, :, cols])
+        if linked:
+
+            @pl.when(turn == 0)
+            def _():
+                gather.pair(1)
+                gather.forward(2)
+                gather.start(3)
 
     if linked:
         net.drain()
@@ -713,7 +714,7 @@
 
     @pl.loop(0, parts)
     def _(turn):
-        m = of_turn(turn)
+        m = of_turn((2 * (turn // 2 + turn % 2 - 2 * (turn // 2) * (turn % 2)) + turn // 2) if linked else turn)
         for first in range(0, fm, fm // 2):
             units_of = slice(first, first + fm // 2)
             up = dot(n2[...], wu[m, :, units_of])
@@ -721,6 +722,17 @@
             cdf, xpdf = gelu_terms(up)
             act[:, units_of] = (up * cdf).astype(bf16)
             dup[:, units_of] = (da * (cdf + xpdf)).astype(bf16)
+            if linked and first == 0:
+
+                @pl.when(turn == 2)
+                def _():
+                    reduce.plane(UPDOWN, 2)
+
+                @pl.when(turn == 3)
+                def _():
+                    reduce.plane(UPDOWN, 3)
+                    reduce.model(UPDOWN, 2)
+
         for cols in column_halves:
             acc_a[:, cols] += dot(act[...], wd[m, :, cols])
         for cols in column_halves:
@@ -732,17 +744,21 @@
             part = slice(c, c + fm // 2)
             stack_turned(m, units[UPDOWN][1] // 2 + c // BLK * (D // BLK), dot(cott[...], act[:, part]))
         if linked:
-            for k in (1, 2, 3):
-
-                @pl.when(turn == k)
-                def _():
-                    if k == 1:
-                        gather.all_done()
-                    reduce.chip(UPDOWN, k)
-                    if k > 1:
-                        reduce.plane(UPDOWN, k - 1)
-                    if k == 3:
-                        reduce.model(UPDOWN, 1)
+
+            @pl.when(turn == 1)
+            def _():
+                gather.all_done()
+                reduce.chip(UPDOWN, 2)
+
+            @pl.when(turn == 2)
+            def _():
+                reduce.chip(UPDOWN, 3)
+                reduce.turn(UPDOWN, 2)
+
+            @pl.when(turn == 3)
+            def _():
+                reduce.chip(UPDOWN, 1)
+                reduce.turn(UPDOWN, 3)
 
     gain_sum_two = jnp.zeros((1, D), f32)
 
@@ -760,7 +776,8 @@
 
     gain_sum_two = lax.fori_loop(0, L // R, back_two, gain_sum_two)
     if linked:
-        reduce.plane(UPDOWN, 3)
+        reduce.plane(UPDOWN, 1)
+        reduce.model(UPDOWN, 3)
     dmlt[...] = dml[...].T
     fetch_tok = pltpu.make_async_copy(tokens, cot, local.at[1])
     fetch_tok.start()
@@ -811,13 +828,15 @@
 
             @pl.when(turn == 3)
             def _():
-                reduce.turn(UPDOWN, 2)
                 for i in (3, 2, 1):
                     reduce.plane(OUT, i)
-
-            @pl.when(turn == 0)
-            def _():
-                reduce.plane(GATE, 1)
+                reduce.model(UPDOWN, 1)
+
+            for k in (2, 1, 0):
+
+                @pl.when(turn == k)
+                def _():
+                    reduce.plane(GATE, k + 1)
 
         @pl.loop(0, L // R)
         def _(i):
@@ -834,28 +853,18 @@
 
         if linked:
 
-            @pl.when(turn == 3)
-            def _():
-                reduce.turn(UPDOWN, 3)
-
             @pl.when(turn == 2)
             def _():
-                reduce.plane(GATE, 3)
-                for i in (3, 2):
-                    reduce.turn(OUT, i)
-                reduce.model(UPDOWN, 3)
-                reduce.model(UPDOWN, 2)
+                for i in (3, 2, 1):
+                    reduce.model(OUT, i)
 
             @pl.when(turn == 1)
             def _():
-                reduce.plane(GATE, 2)
-                for i in (1, 3, 2):
-                    reduce.model(OUT, i)
+                reduce.model(GATE, 3)
 
             @pl.when(turn == 0)
             def _():
-                reduce.turn(GATE, 2)
-                reduce.model(GATE, 3)
+                reduce.model(GATE, 2)
 
         for k in range(3):
             stack(m, units[GATE][0], 3 * hm // BLK, k * hm // BLK, dot(n1t[...], dpre[:, k * hm : (k + 1) * hm]))
@@ -868,19 +877,19 @@
                 @pl.when(turn == k)
                 def _():
                     reduce.chip(GATE, k)
-                    if k == 1:
-                        reduce.turn(GATE, 3)
+                    if k == 3:
+                        reduce.turn(OUT, 3)
+                        reduce.turn(OUT, 2)
+                    else:
+                        reduce.turn(GATE, k + 1)
 
     if linked:
         reduce.own(UPDOWN)
         reduce.own(OUT)
+        reduce.model(GATE, 1)
 
     fetch_tok.wait()
     permute_in(cot, cot)
-    if linked:
-        reduce.model(GATE, 1)
-        reduce.model(GATE, 2)
-
     def back_one(i, total):
         rows = pl.ds(pl.multiple_of(i * R, R), R)
         x = cot[rows, :].astype(f32)

time: 130 us -> 128 us (0.985)
  Pallas kernels: 129 us -> 127 us
    pallas_call x1, Pallas kernels: 123 us -> 121 us  [compute(): pl.pallas_call(functools.partial(compute_kernel, linked), out_shape=(sds(...]
where the time goes in v4:
time: 128 us
  Pallas kernels  127 us (99%)
    pallas_call x1, Pallas kernels, compute(): pl.pallas_call(functools.partial(compute_kernel, linked), out_shape=(sds(...  121 us
    pallas_call x1, Pallas kernels, update(): pl.pallas_call(functools.partial(update_kernel, token_total, len(passed))...  6.42 us

profile of v4, /device:TPU:0, one launch (start us, length us, event | category | flops | bytes accessed | tf_op | source)
XLA Modules:
  0.0 128.0 jit_solution(7348582998242866831)
XLA Ops:
  0.6 120.7 %block.1 = (bf16[1024,512]{1,0:T(8,128)(2,1)}, f32[1024,512]{1,0:T(8,128)}, f32[8,128,128]{2,1,0:T(8,128)}, f32[8,512]{1,0:T(8,128)}) custom-call(bf16[1024,512]{1,0:T(8,128)(2,1)} %refs_0_.1, bf16[1024,512]{1,0:T(8,128)(2,1)} %refs_1_.1, f32[8,128,128]{2,1,0:T(8,128)} %bitcast.10, s32[64]{0:T(128)} %refs_3_.1, f32[2,512]{1,0:T(2,128)} %gains.1), custom_call_target="tpu_custom_call" | custom-call | tf_op jit(solution)/shard_map/block/pallas_call | solution.py:992
  121.4 6.4 %update.1 = (f32[8,128,128]{2,1,0:T(8,128)}, f32[8,128,128]{2,1,0:T(8,128)}, f32[8,128,128]{2,1,0:T(8,128)}, bf16[8,128,128]{2,1,0:T(8,128)(2,1)}, f32[2,512]{1,...) custom-call(f32[8,512]{1,0:T(8,128)} %get-tuple-element.24.sums, ...), custom_call_target="tpu_custom_call" | custom-call | tf_op jit(solution)/shard_map/update/pallas_call | solution.py:1097

commit v5 on v4

--- a/solution.py
+++ b/solution.py
@@ -731,7 +731,6 @@
                 @pl.when(turn == 3)
                 def _():
                     reduce.plane(UPDOWN, 3)
-                    reduce.model(UPDOWN, 2)
 
         for cols in column_halves:
             acc_a[:, cols] += dot(act[...], wd[m, :, cols])
@@ -759,6 +758,7 @@
             def _():
                 reduce.chip(UPDOWN, 1)
                 reduce.turn(UPDOWN, 3)
+                reduce.model(UPDOWN, 2)
 
     gain_sum_two = jnp.zeros((1, D), f32)
 
@@ -777,7 +777,6 @@
     gain_sum_two = lax.fori_loop(0, L // R, back_two, gain_sum_two)
     if linked:
         reduce.plane(UPDOWN, 1)
-        reduce.model(UPDOWN, 3)
     dmlt[...] = dml[...].T
     fetch_tok = pltpu.make_async_copy(tokens, cot, local.at[1])
     fetch_tok.start()
@@ -789,6 +788,7 @@
     if linked:
         for i in (3, 2, 1):
             reduce.chip(OUT, i)
+        reduce.model(UPDOWN, 3)
 
     def keeps(m, rows):
         f = forget[m, rows, :]
@@ -830,13 +830,17 @@
             def _():
                 for i in (3, 2, 1):
                     reduce.plane(OUT, i)
-                reduce.model(UPDOWN, 1)
 
             for k in (2, 1, 0):
 
                 @pl.when(turn == k)
                 def _():
                     reduce.plane(GATE, k + 1)
+                    if k == 2:
+                        reduce.turn(OUT, 3)
+                        reduce.turn(OUT, 2)
+                    else:
+                        reduce.turn(GATE, k + 2)
 
         @pl.loop(0, L // R)
         def _(i):
@@ -851,21 +855,6 @@
             dpre[rows, 2 * hm :] = (carried * adm).astype(bf16)
             keeps(m_next, rows)
 
-        if linked:
-
-            @pl.when(turn == 2)
-            def _():
-                for i in (3, 2, 1):
-                    reduce.model(OUT, i)
-
-            @pl.when(turn == 1)
-            def _():
-                reduce.model(GATE, 3)
-
-            @pl.when(turn == 0)
-            def _():
-                reduce.model(GATE, 2)
-
         for k in range(3):
             stack(m, units[GATE][0], 3 * hm // BLK, k * hm // BLK, dot(n1t[...], dpre[:, k * hm : (k + 1) * hm]))
         for cols in column_halves:
@@ -878,15 +867,18 @@
                 def _():
                     reduce.chip(GATE, k)
                     if k == 3:
-                        reduce.turn(OUT, 3)
-                        reduce.turn(OUT, 2)
-                    else:
-                        reduce.turn(GATE, k + 1)
-
-    if linked:
+                        reduce.model(UPDOWN, 1)
+                    if k == 2:
+                        for i in (3, 2, 1):
+                            reduce.model(OUT, i)
+                    if k == 1:
+                        reduce.model(GATE, 3)
+
+    if linked:
+        reduce.model(GATE, 2)
         reduce.own(UPDOWN)
+        reduce.model(GATE, 1)
         reduce.own(OUT)
-        reduce.model(GATE, 1)
 
     fetch_tok.wait()
     permute_in(cot, cot)

time: 128 us -> 128 us (level)
  no operation moved by 1% of the time
where the time goes in v5:
time: 128 us
  Pallas kernels  127 us (99%)
    pallas_call x1, Pallas kernels, compute(): pl.pallas_call(functools.partial(compute_kernel, linked), out_shape=(sds(...  121 us
    pallas_call x1, Pallas kernels, update(): pl.pallas_call(functools.partial(update_kernel, token_total, len(passed))...  6.42 us

profile of v5, /device:TPU:0, one launch (start us, length us, event | category | flops | bytes accessed | tf_op | source)
XLA Modules:
  0.0 128.1 jit_solution(3809806811031875475)
XLA Ops:
  0.6 120.8 %block.1 = (bf16[1024,512]{1,0:T(8,128)(2,1)}, f32[1024,512]{1,0:T(8,128)}, f32[8,128,128]{2,1,0:T(8,128)}, f32[8,512]{1,0:T(8,128)}) custom-call(bf16[1024,512]{1,0:T(8,128)(2,1)} %refs_0_.1, bf16[1024,512]{1,0:T(8,128)(2,1)} %refs_1_.1, f32[8,128,128]{2,1,0:T(8,128)} %bitcast.10, s32[64]{0:T(128)} %refs_3_.1, f32[2,512]{1,0:T(2,128)} %gains.1), custom_call_target="tpu_custom_call" | custom-call | tf_op jit(solution)/shard_map/block/pallas_call | solution.py:984
  121.5 6.4 %update.1 = (f32[8,128,128]{2,1,0:T(8,128)}, f32[8,128,128]{2,1,0:T(8,128)}, f32[8,128,128]{2,1,0:T(8,128)}, bf16[8,128,128]{2,1,0:T(8,128)(2,1)}, f32[2,512]{1,...) custom-call(f32[8,512]{1,0:T(8,128)} %get-tuple-element.24.sums, ...), custom_call_target="tpu_custom_call" | custom-call | tf_op jit(solution)/shard_map/update/pallas_call | solution.py:1089

commit v6 on v5

--- a/solution.py
+++ b/solution.py
@@ -252,11 +252,13 @@
 
 
 UPDOWN, OUT, GATE = range(3)
+REST = 1
 
 
 class Reduce:
     def __init__(self, net, gather, grads, units, pool):
-        self.net, self.g, self.grads, self.units, self.pool = net, gather, grads, units, pool
+        self.net, self.g, self.grads, self.pool = net, gather, grads, pool
+        self.units = (units[UPDOWN], (units[OUT][0], units[OUT][1] + units[GATE][1]))
         self.half = grads.shape[1] // 2
         self.eighth = grads.shape[1] // 8
 
@@ -281,33 +283,16 @@
         base, total = self.units[unit]
         return self.pool[i - 1].at[pl.ds(self.half + slot * self.eighth + base // 8 + first, count)]
 
-    def parts(self, unit, i):
-        n = self.units[unit][1] // 8
-        if i == 1:
-            return ((0, n),)
-        h = (n + i % 2) // 2 if n % 2 else n // 2
-        return (0, h), (h, n - h)
-
     def share(self, unit, i, e, first, count):
         base, total = self.units[unit]
         return self.grads.at[self.g.order[i], pl.ds(base + self.place(e) * (total // 8) + first, count)]
 
-    def over(self, unit, i, slot, part):
-        x, y, z = self.g.plane
-        e = (z, x, y)[slot]
-        to = (x if part == self.parts(unit, i)[0] else y, x, y)[slot]
+    def over(self, unit, i, k):
+        n = self.units[unit][1] // 8
+        e = self.g.plane[k]
         return self.net.copy(
-            lambda: (self.share(unit, i, e, *part), self.spot(unit, i, slot, *part), (to, self.g.m)),
-            ("over", unit, i, slot, part),
+            lambda: (self.share(unit, i, e, 0, n), self.spot(unit, i, k, 0, n), (e, self.g.m)), ("over", unit, i, k)
         )
-
-    def send(self, unit, i, slot, part):
-        if part[1]:
-            self.over(unit, i, slot, part).start()
-
-    def take(self, unit, i, slot, part):
-        self.over(unit, i, slot, part).wait_recv()
-        return self.spot(unit, i, slot, *part)[...].astype(f32)
 
     def model_copy(self, unit, i):
         n = self.units[unit][1] // 8
@@ -321,7 +306,7 @@
         return self.net.copy(
             lambda: (
                 self.share(unit, 1, self.g.plane[2], *part),
-                self.spot(unit, 1, 0, *part),
+                self.spot(unit, 1, 2, *part),
                 (self.g.me, self.g.order[1]),
             ),
             ("aside", unit),
@@ -334,41 +319,24 @@
         m = g.order[i]
         start, came = first + g.side * (count // 2), self.pool[i - 1]
 
-        @pl.loop(0, count // 2)
+        @pl.loop(0, count // 2, unroll=4)
         def _(b):
             total = self.grads[m, start + b].astype(f32) + came[first // 2 + b].astype(f32)
             self.grads[m, start + b] = total.astype(bf16)
 
+        for k in range(2 if i == 1 else 3):
+            self.over(unit, i, k).start()
         if i == 1:
-            (whole,) = self.parts(unit, i)
-            self.send(unit, i, 1, whole)
-            self.send(unit, i, 2, whole)
             self.aside(unit).start()
-            return
-        one, two = self.parts(unit, i)
-        self.send(unit, i, 0, one)
-        self.send(unit, i, 0, two)
-        self.send(unit, i, 1, one)
-        self.send(unit, i, 2, two)
-
-    def turn(self, unit, i):
-        if i == 1:
-            return
-        x, y, _ = self.g.plane
-        for part, slot, e in zip(self.parts(unit, i), (2, 1), (y, x)):
-            if part[1]:
-                ref = self.share(unit, i, e, *part)
-                ref[...] = (ref[...].astype(f32) + self.take(unit, i, 0, part)).astype(bf16)
-                self.send(unit, i, slot, part)
 
     def model(self, unit, i):
-        g, (first, count) = self.g, self.units[unit]
-        n = count // 8
-        for part in self.parts(unit, i):
-            if part[1]:
-                ref = self.share(unit, i, g.me, *part)
-                total = ref[...].astype(f32) + self.take(unit, i, 1, part) + self.take(unit, i, 2, part)
-                ref[...] = total.astype(bf16)
+        n = self.units[unit][1] // 8
+        ref = self.share(unit, i, self.g.me, 0, n)
+        total = ref[...].astype(f32)
+        for k in range(2 if i == 1 else 3):
+            self.over(unit, i, k).wait_recv()
+            total += self.spot(unit, i, k, 0, n)[...].astype(f32)
+        ref[...] = total.astype(bf16)
         self.model_copy(unit, i).start()
 
     def own(self, unit):
@@ -382,7 +350,7 @@
         self.grads[g.m, rows] = total.astype(bf16)
         self.aside(unit).wait_recv()
         rows = pl.ds(first + self.place(g.plane[2]) * n, n)
-        total = self.grads[g.m, rows].astype(f32) + self.spot(unit, 1, 0, 0, n)[...].astype(f32)
+        total = self.grads[g.m, rows].astype(f32) + self.spot(unit, 1, 2, 0, n)[...].astype(f32)
         self.grads[g.m, rows] = total.astype(bf16)
 
     def into_slots(self, out, slot_place, e):
@@ -752,12 +720,10 @@
             @pl.when(turn == 2)
             def _():
                 reduce.chip(UPDOWN, 3)
-                reduce.turn(UPDOWN, 2)
 
             @pl.when(turn == 3)
             def _():
                 reduce.chip(UPDOWN, 1)
-                reduce.turn(UPDOWN, 3)
                 reduce.model(UPDOWN, 2)
 
     gain_sum_two = jnp.zeros((1, D), f32)
@@ -786,8 +752,6 @@
         stack_turned(m, units[OUT][0], dot(dmlt[...], state[m, SUB:, :].astype(bf16)))
 
     if linked:
-        for i in (3, 2, 1):
-            reduce.chip(OUT, i)
         reduce.model(UPDOWN, 3)
 
     def keeps(m, rows):
@@ -828,19 +792,13 @@
 
             @pl.when(turn == 3)
             def _():
-                for i in (3, 2, 1):
-                    reduce.plane(OUT, i)
+                reduce.model(UPDOWN, 1)
 
             for k in (2, 1, 0):
 
                 @pl.when(turn == k)
                 def _():
-                    reduce.plane(GATE, k + 1)
-                    if k == 2:
-                        reduce.turn(OUT, 3)
-                        reduce.turn(OUT, 2)
-                    else:
-                        reduce.turn(GATE, k + 2)
+                    reduce.plane(REST, k + 1)
 
         @pl.loop(0, L // R)
         def _(i):
@@ -865,20 +823,14 @@
 
                 @pl.when(turn == k)
                 def _():
-                    reduce.chip(GATE, k)
-                    if k == 3:
-                        reduce.model(UPDOWN, 1)
-                    if k == 2:
-                        for i in (3, 2, 1):
-                            reduce.model(OUT, i)
+                    reduce.chip(REST, k)
                     if k == 1:
-                        reduce.model(GATE, 3)
-
-    if linked:
-        reduce.model(GATE, 2)
+                        reduce.model(REST, 3)
+
+    if linked:
+        reduce.model(REST, 2)
         reduce.own(UPDOWN)
-        reduce.model(GATE, 1)
-        reduce.own(OUT)
+        reduce.model(REST, 1)
 
     fetch_tok.wait()
     permute_in(cot, cot)
@@ -920,7 +872,7 @@
     if linked:
         tiny = SmallSum(net, gather, small, sum_a, sum_b, sum_c)
         tiny.send(0)
-        reduce.own(GATE)
+        reduce.own(REST)
         reduce.slots_chip(slots, slot_place, pair)
         tiny.add(0)
         tiny.send(1)

time: 128 us -> 130 us (1.016)
  Pallas kernels: 127 us -> 129 us
    pallas_call x1, Pallas kernels: 121 us -> 122 us  [compute(): pl.pallas_call(functools.partial(compute_kernel, linked), out_shape=(sds(...]
where the time goes in v6:
time: 130 us; the launch traced here: 129 us
  Pallas kernels  129 us (99%)
    pallas_call x1, Pallas kernels, compute(): pl.pallas_call(functools.partial(compute_kernel, linked), out_shape=(sds(...  122 us
    pallas_call x1, Pallas kernels, update(): pl.pallas_call(functools.partial(update_kernel, token_total, len(passed))...  6.42 us

profile of v6, /device:TPU:0, one launch (start us, length us, event | category | flops | bytes accessed | tf_op | source)
XLA Modules:
  0.0 129.5 jit_solution(15676457925172253715)
XLA Ops:
  0.6 122.3 %block.1 = (bf16[1024,512]{1,0:T(8,128)(2,1)}, f32[1024,512]{1,0:T(8,128)}, f32[8,128,128]{2,1,0:T(8,128)}, f32[8,512]{1,0:T(8,128)}) custom-call(bf16[1024,512]{1,0:T(8,128)(2,1)} %refs_0_.1, bf16[1024,512]{1,0:T(8,128)(2,1)} %refs_1_.1, f32[8,128,128]{2,1,0:T(8,128)} %bitcast.10, s32[64]{0:T(128)} %refs_3_.1, f32[2,512]{1,0:T(2,128)} %gains.1), custom_call_target="tpu_custom_call" | custom-call | tf_op jit(solution)/shard_map/block/pallas_call | solution.py:936
  122.9 6.4 %update.1 = (f32[8,128,128]{2,1,0:T(8,128)}, f32[8,128,128]{2,1,0:T(8,128)}, f32[8,128,128]{2,1,0:T(8,128)}, bf16[8,128,128]{2,1,0:T(8,128)(2,1)}, f32[2,512]{1,...) custom-call(f32[8,512]{1,0:T(8,128)} %get-tuple-element.24.sums, ...), custom_call_target="tpu_custom_call" | custom-call | tf_op jit(solution)/shard_map/update/pallas_call | solution.py:1041

commit v7 on v5

--- a/solution.py
+++ b/solution.py
@@ -281,9 +281,12 @@
         base, total = self.units[unit]
         return self.pool[i - 1].at[pl.ds(self.half + slot * self.eighth + base // 8 + first, count)]
 
+    def direct(self, unit, i):
+        return i == 1 or unit == UPDOWN
+
     def parts(self, unit, i):
         n = self.units[unit][1] // 8
-        if i == 1:
+        if self.direct(unit, i):
             return ((0, n),)
         h = (n + i % 2) // 2 if n % 2 else n // 2
         return (0, h), (h, n - h)
@@ -295,7 +298,8 @@
     def over(self, unit, i, slot, part):
         x, y, z = self.g.plane
         e = (z, x, y)[slot]
-        to = (x if part == self.parts(unit, i)[0] else y, x, y)[slot]
+        by = z if self.direct(unit, i) else x if part == self.parts(unit, i)[0] else y
+        to = (by, x, y)[slot]
         return self.net.copy(
             lambda: (self.share(unit, i, e, *part), self.spot(unit, i, slot, *part), (to, self.g.m)),
             ("over", unit, i, slot, part),
@@ -334,16 +338,19 @@
         m = g.order[i]
         start, came = first + g.side * (count // 2), self.pool[i - 1]
 
-        @pl.loop(0, count // 2)
+        @pl.loop(0, count // 2, unroll=4)
         def _(b):
             total = self.grads[m, start + b].astype(f32) + came[first // 2 + b].astype(f32)
             self.grads[m, start + b] = total.astype(bf16)
 
-        if i == 1:
+        if self.direct(unit, i):
             (whole,) = self.parts(unit, i)
             self.send(unit, i, 1, whole)
             self.send(unit, i, 2, whole)
-            self.aside(unit).start()
+            if i == 1:
+                self.aside(unit).start()
+            else:
+                self.send(unit, i, 0, whole)
             return
         one, two = self.parts(unit, i)
         self.send(unit, i, 0, one)
@@ -352,7 +359,7 @@
         self.send(unit, i, 2, two)
 
     def turn(self, unit, i):
-        if i == 1:
+        if self.direct(unit, i):
             return
         x, y, _ = self.g.plane
         for part, slot, e in zip(self.parts(unit, i), (2, 1), (y, x)):
@@ -368,6 +375,8 @@
             if part[1]:
                 ref = self.share(unit, i, g.me, *part)
                 total = ref[...].astype(f32) + self.take(unit, i, 1, part) + self.take(unit, i, 2, part)
+                if i > 1 and self.direct(unit, i):
+                    total += self.take(unit, i, 0, part)
                 ref[...] = total.astype(bf16)
         self.model_copy(unit, i).start()
 

time: 128 us -> 129 us (level)
  no operation moved by 1% of the time
where the time goes in v7:
time: 129 us; the launch traced here: 128 us
  Pallas kernels  128 us (99%)
    pallas_call x1, Pallas kernels, compute(): pl.pallas_call(functools.partial(compute_kernel, linked), out_shape=(sds(...  121 us
    pallas_call x1, Pallas kernels, update(): pl.pallas_call(functools.partial(update_kernel, token_total, len(passed))...  6.42 us

profile of v7, /device:TPU:0, one launch (start us, length us, event | category | flops | bytes accessed | tf_op | source)
XLA Modules:
  0.0 128.4 jit_solution(687226439979364490)
XLA Ops:
  0.6 121.2 %block.1 = (bf16[1024,512]{1,0:T(8,128)(2,1)}, f32[1024,512]{1,0:T(8,128)}, f32[8,128,128]{2,1,0:T(8,128)}, f32[8,512]{1,0:T(8,128)}) custom-call(bf16[1024,512]{1,0:T(8,128)(2,1)} %refs_0_.1, bf16[1024,512]{1,0:T(8,128)(2,1)} %refs_1_.1, f32[8,128,128]{2,1,0:T(8,128)} %bitcast.10, s32[64]{0:T(128)} %refs_3_.1, f32[2,512]{1,0:T(2,128)} %gains.1), custom_call_target="tpu_custom_call" | custom-call | tf_op jit(solution)/shard_map/block/pallas_call | solution.py:993
  121.9 6.4 %update.1 = (f32[8,128,128]{2,1,0:T(8,128)}, f32[8,128,128]{2,1,0:T(8,128)}, f32[8,128,128]{2,1,0:T(8,128)}, bf16[8,128,128]{2,1,0:T(8,128)(2,1)}, f32[2,512]{1,...) custom-call(f32[8,512]{1,0:T(8,128)} %get-tuple-element.24.sums, ...), custom_call_target="tpu_custom_call" | custom-call | tf_op jit(solution)/shard_map/update/pallas_call | solution.py:1098

commit v8 on v4

--- a/solution.py
+++ b/solution.py
@@ -334,7 +334,7 @@
         m = g.order[i]
         start, came = first + g.side * (count // 2), self.pool[i - 1]
 
-        @pl.loop(0, count // 2)
+        @pl.loop(0, count // 2, unroll=4)
         def _(b):
             total = self.grads[m, start + b].astype(f32) + came[first // 2 + b].astype(f32)
             self.grads[m, start + b] = total.astype(bf16)
@@ -409,7 +409,7 @@
         for e in targets:
             self.into_slots(out, slot_place, e)
 
-    def slots_plane(self, out, pair, far):
+    def slots_plane(self, out, pair, far, meanwhile):
         g, n = self.g, out.shape[0] // 8
         h = n // 2
         x, y, z = g.plane
@@ -435,6 +435,7 @@
         wait["y"].wait_recv()
         join(y)
         self.ends.append(send(y, h, 3, y))
+        meanwhile()
         over_x.wait_recv()
         rows = mine(y, 0, h)
         out[rows] = (out[rows].astype(f32) + far[0].astype(f32)).astype(bf16)
@@ -885,8 +886,8 @@
 
     if linked:
         reduce.own(UPDOWN)
+        reduce.model(GATE, 1)
         reduce.own(OUT)
-        reduce.model(GATE, 1)
 
     fetch_tok.wait()
     permute_in(cot, cot)
@@ -901,9 +902,11 @@
 
     gain_sum_one = lax.fori_loop(0, L // R, back_one, jnp.zeros((1, D), f32))
 
-    permute_out(acc_a, n1)
     push_out = pltpu.make_async_copy(n1, block_out, local.at[0])
-    push_out.start()
+
+    def finish_block_out():
+        permute_out(acc_a, n1)
+        push_out.start()
 
     place = lax.broadcasted_iota(jnp.int32, (SUB, hm), 0).astype(f32) * float(J)
     if linked:
@@ -932,7 +935,9 @@
         reduce.slots_chip(slots, slot_place, pair)
         tiny.add(0)
         tiny.send(1)
-        reduce.slots_plane(slots, pair, far)
+        reduce.slots_plane(slots, pair, far, finish_block_out)
+    else:
+        finish_block_out()
 
     permute_out(mixed, acc_a)
     push_grad = pltpu.make_async_copy(acc_a, input_grad, local.at[2])

time: 128 us -> 128 us (level)
  no operation moved by 1% of the time
where the time goes in v8:
time: 128 us
  Pallas kernels  127 us (99%)
    pallas_call x1, Pallas kernels, compute(): pl.pallas_call(functools.partial(compute_kernel, linked), out_shape=(sds(...  121 us
    pallas_call x1, Pallas kernels, update(): pl.pallas_call(functools.partial(update_kernel, token_total, len(passed))...  6.43 us

profile of v8, /device:TPU:0, one launch (start us, length us, event | category | flops | bytes accessed | tf_op | source)
XLA Modules:
  0.0 127.8 jit_solution(1856613290454902484)
XLA Ops:
  0.6 120.6 %block.1 = (bf16[1024,512]{1,0:T(8,128)(2,1)}, f32[1024,512]{1,0:T(8,128)}, f32[8,128,128]{2,1,0:T(8,128)}, f32[8,512]{1,0:T(8,128)}) custom-call(bf16[1024,512]{1,0:T(8,128)(2,1)} %refs_0_.1, bf16[1024,512]{1,0:T(8,128)(2,1)} %refs_1_.1, f32[8,128,128]{2,1,0:T(8,128)} %bitcast.10, s32[64]{0:T(128)} %refs_3_.1, f32[2,512]{1,0:T(2,128)} %gains.1), custom_call_target="tpu_custom_call" | custom-call | tf_op jit(solution)/shard_map/block/pallas_call | solution.py:997
  121.3 6.4 %update.1 = (f32[8,128,128]{2,1,0:T(8,128)}, f32[8,128,128]{2,1,0:T(8,128)}, f32[8,128,128]{2,1,0:T(8,128)}, bf16[8,128,128]{2,1,0:T(8,128)(2,1)}, f32[2,512]{1,...) custom-call(f32[8,512]{1,0:T(8,128)} %get-tuple-element.24.sums, ...), custom_call_target="tpu_custom_call" | custom-call | tf_op jit(solution)/shard_map/update/pallas_call | solution.py:1102
